TPU v7x, 32 devices: a whole 2x2x4 slice. The times are simulated.
32 devices in a mesh: lat: 4 (over z), lon: 8 (over y, x, core).
Axes of the slice: x: 2, y: 2, z: 4, core: 2. Of those that a mesh axis runs over, the one named last changes fastest.
Arguments:
- state: bfloat16 [256, 1440, 320], P('lat', 'lon'), may hold values from -6 to 6
- cutoff: int32 [128], replicated, may hold values from 90 to 719
- viscosity: float32 [320], replicated, may hold values from 0.02 to 0.2
Outputs:
- updated: float32 [256, 1440, 320], P('lat', 'lon')
All inputs are finite; a program needn't handle non-finite values.
Results may differ from a plain program's by a relative error of at most 0.0033.
Values may be sent and summed in bfloat16 or wider, within the bound.
No kernel may reach another device: no remote copies, remote signals or barrier semaphores. Data moves between devices by JAX's collectives and lax.ppermute only.
A program may use at most 128 MiB of HBM per device.

v0:
```python
import math

import jax
import jax.numpy as jnp
from jax import lax
from jax.sharding import PartitionSpec as P

NLON = 1440


def with_halo(cells, sides, width, closed):
    for axis, dim in sides:
        count = lax.axis_size(axis)
        ends = count if closed else count - 1
        head = lax.slice_in_dim(cells, 0, width, axis=dim)
        tail = lax.slice_in_dim(cells, cells.shape[dim] - width, cells.shape[dim], axis=dim)
        cells = jnp.concatenate(
            [
                lax.ppermute(tail, axis, [(i, (i + 1) % count) for i in range(ends)]),
                cells,
                lax.ppermute(head, axis, [((i + 1) % count, i) for i in range(ends)]),
            ],
            axis=dim,
        )
    return cells


def fourier_table(length):
    column = jnp.arange(length, dtype=jnp.int32)
    half_len = length // 2
    wavenumber = jnp.where(column <= half_len, column, column - half_len)
    product = column[:, None] * wavenumber[None, :] % length
    angles = product.astype(jnp.float32) * jnp.float32(2.0 * math.pi / length)
    fourier = jnp.where((column <= half_len)[None, :], jnp.cos(angles), jnp.sin(angles))
    weights = jnp.where(
        (column == 0) | (column == half_len), jnp.float32(1.0 / length), jnp.float32(2.0 / length)
    )
    return (fourier.astype(jnp.bfloat16), wavenumber, weights)


def filter_block(row_block, cut_rows, fourier, wavenumber, weights):
    spectrum = jnp.einsum("jk,rjc->rkc", fourier, row_block, preferred_element_type=jnp.float32)
    retain = (wavenumber[None, :] <= cut_rows[:, None]).astype(jnp.float32) * weights[None, :]
    damped = (spectrum * retain[:, :, None]).astype(jnp.bfloat16)
    result = jnp.einsum("jk,rkc->rjc", fourier, damped, preferred_element_type=jnp.float32)
    return result.astype(jnp.bfloat16)


def metric(global_rows, nlat):
    spacing = jnp.float32(math.pi / nlat)
    rows_f = global_rows.astype(jnp.float32)
    cell_cos = jnp.sin((rows_f + 0.5) * spacing)
    north_cos = jnp.where(global_rows == 0, jnp.float32(0.0), jnp.sin(rows_f * spacing))
    south_cos = jnp.where(
        global_rows == nlat - 1, jnp.float32(0.0), jnp.sin((rows_f + 1.0) * spacing)
    )
    return (north_cos / cell_cos, south_cos / cell_cos)


def rim_fields(filtered):
    side_cols = with_halo(filtered, (("lon", 1),), 1, True)
    side_rows = with_halo(filtered, (("lat", 0),), 1, False)
    west_q = side_cols[:, :-2].astype(jnp.float32)
    east_q = side_cols[:, 2:].astype(jnp.float32)
    north_q = side_rows[:-2].astype(jnp.float32)
    south_q = side_rows[2:].astype(jnp.float32)
    return (west_q, east_q, north_q, south_q)


def per_device(state, cutoff, viscosity):
    rows_tile, cols_tile, channels = state.shape
    lat_count = lax.axis_size("lat")
    lon_count = lax.axis_size("lon")
    nlat = rows_tile * lat_count
    quarter = nlat // 4
    lat_pos = lax.axis_index("lat")
    lon_pos = lax.axis_index("lon")
    band_rows = rows_tile // lon_count
    fourier, wavenumber, weights = fourier_table(NLON)
    edge_tiles = lat_count // 4
    is_polar = (lat_pos < edge_tiles) | (lat_pos >= lat_count - edge_tiles)
    polar_count = cutoff.shape[0]

    def lookup(global_rows):
        polar_index = jnp.where(global_rows < quarter, global_rows, global_rows - nlat // 2)
        matches = jnp.arange(polar_count, dtype=jnp.int32)[None, :] == polar_index[:, None]
        return jnp.sum(jnp.where(matches, cutoff[None, :], 0), axis=1)

    def apply_filter(row_block, global_rows):
        return filter_block(row_block, lookup(global_rows), fourier, wavenumber, weights)

    own_rows = lat_pos * rows_tile + lon_pos * band_rows + jnp.arange(band_rows, dtype=jnp.int32)

    def polar_branch(block_rows):
        return apply_filter(block_rows, own_rows)

    def plain_branch(block_rows):
        return block_rows

    full_rows = lax.all_to_all(state, "lon", split_axis=0, concat_axis=1, tiled=True)
    full_rows = lax.cond(is_polar, polar_branch, plain_branch, full_rows)
    filtered = lax.all_to_all(full_rows, "lon", split_axis=1, concat_axis=0, tiled=True)
    west_q, east_q, north_q, south_q = rim_fields(filtered)
    fields = filtered.astype(jnp.float32)
    tile_rows = lat_pos * rows_tile + jnp.arange(rows_tile, dtype=jnp.int32)
    north_ratio, south_ratio = metric(tile_rows, nlat)
    viscous = viscosity[None, None, :]
    updated = fields + viscous * (east_q - 2.0 * fields + west_q)
    updated = updated + viscous * (
        north_ratio[:, None, None] * (north_q - fields)
        - south_ratio[:, None, None] * (fields - south_q)
    )
    return updated


def solution(mesh):
    in_specs = (P("lat", "lon", None), P(), P())
    out_specs = P("lat", "lon", None)
    return jax.shard_map(
        per_device, mesh=mesh, in_specs=in_specs, out_specs=out_specs, check_vma=False
    )
```

profile of v0, /device:TPU:0, one launch (start us, length us, event | category | flops | bytes accessed | tf_op | source)
XLA Modules:
  0.0 333.9 jit_solution(15856090198620979385)
XLA Ops:
  0.0 12.4 %copy.23 = bf16[64,180,320]{2,1,0:T(8,128)(2,1)} copy(bf16[64,180,320]{2,0,1:T(8,128)(2,1)} %param.5) | data formatting | bytes 14745600 | tf_op args[0]
  12.4 5.2 %all-to-all-start = ((bf16[64,180,320]{2,1,0:T(8,128)(2,1)}), bf16[64,180,320]{2,1,0:T(8,128)(2,1)}, u32[]{:S(2)}, u32[]{:S(2)}) async-start(bf16[64,180,320]{2,1,0:T(8,128)(2,1)} %copy.23), calls=%async_computation | async-start | bytes 18087936 | tf_op jit(solution)/shard_map/all_to_all | solution.py:100
  17.6 38.7 %select_convert_fusion = bf16[1440,1440]{1,0:T(8,128)(2,1)} fusion(s32[1440]{0:T(1024)S(1)} %add_select_fusion.1, pred[1440]{0:T(1024)(128)(4,1)S(1)} %iota_compare_fusion.1), kind=kLoop, calls=%fused_computation.35 | loop fusion | flops 22809600 | bytes 4154400 | tf_op jit(solution)/shard_map/convert_element_type | solution.py:38
  56.3 62.9 %all-to-all-done = bf16[64,180,320]{2,1,0:T(8,128)(2,1)} async-done(((bf16[64,180,320]{2,1,0:T(8,128)(2,1)}), bf16[64,180,320]{2,1,0:T(8,128)(2,1)}, u32[]{:S(2)}, u32[]{:S(2)}) %all-to-all-start) | async-done | bytes 7372832 | tf_op jit(solution)/shard_map/all_to_all | solution.py:100
  119.2 8.3 %copy.24 = bf16[8,8,180,320]{3,1,2,0:T(8,128)(2,1)} copy(bf16[8,8,180,320]{3,2,1,0:T(8,128)(2,1)} %bitcast.4) | data formatting | bytes 14745600 | tf_op jit(solution)/shard_map/all_to_all | solution.py:100
  127.5 36.1 %conditional.1 = (bf16[8,1440,320]{1,2,0:T(8,128)(2,1)}) conditional(s32[]{:T(128)} %convert_element_type.53, (bf16[8,1440,320]{2,0,1:T(8,128)(2,1)}) %tuple.34, (bf16[8,1440,320]{2,0,1:T(8,128)(2,1)}, bf16[1440,1440]{1,0:T(8,128)(2,1)}, s32[1440]{0:T(1024)S(1)}, s32[1440]{0:T(1024)S(1)}, s32[]{:T(128)}, /*index=5*/s32[]{:T(128)}, s32[8]{0:T(128)S(1)}, ...), branch_computations={%region_0.1_spmd, %region_1.3_spmd} | conditional | flops 21244760064 | bytes 23178948 | solution.py:101
  127.7 0.2 select_reduce_fusion
  127.9 0.1 compare_select_fusion
  128.0 35.6 %convert_bitcast_fusion = bf16[8,1440,320]{1,2,0:T(8,128)(2,1)} fusion(bf16[8,1440,320]{2,0,1:T(8,128)(2,1)} %get-tuple-element.123, f32[8,1440]{1,0:T(8,128)S(1)} %compare_select_fusion, bf16[1440,1440]{1,0:T(8,128)(2,1)} %get-tuple-element.90, bf16[1440,1440]{1,0:T(8,128)(2,1)} %get-tuple-element.90), kind=kOutput, calls=%fused_computation.5 | convolution fusion | flops 21244723200 | bytes 23086080 | tf_op jit(solution)/shard_map/cond/branch_1_fun/jk,rkc->rjc/dot_general | solution.py:45
  163.5 12.1 %copy.27 = bf16[8,1440,320]{2,0,1:T(8,128)(2,1)} copy(bf16[8,1440,320]{1,2,0:T(8,128)(2,1)} %get-tuple-element.141) | data formatting | bytes 14745600 | tf_op jit(solution)/shard_map/cond | solution.py:101
  175.7 104.8 %all_to_all.39 = bf16[8,1440,320]{2,0,1:T(8,128)(2,1)} all-to-all(bf16[8,1440,320]{2,0,1:T(8,128)(2,1)} %copy.27), channel_id=1, replica_groups=mesh['lat'=4,'lon'=8] {'lon'}, dimensions={1} | all-to-all | bytes 14745600 | tf_op jit(solution)/shard_map/all_to_all | solution.py:102
  280.5 8.7 %copy.39 = bf16[8,8,180,320]{3,1,0,2:T(8,128)(2,1)} copy(bf16[8,8,180,320]{3,1,2,0:T(8,128)(2,1)} %bitcast.29) | data formatting | bytes 14745600 | tf_op jit(solution)/shard_map/all_to_all | solution.py:102
  289.2 2.0 fusion.33
  291.2 1.3 collective-permute-start.2
  292.5 1.3 collective-permute-start.3
  293.8 0.8 fusion.32
  294.6 0.1 collective-permute-start
  294.7 0.5 collective-permute-start.1
  295.2 0.1 fusion.30
  295.3 1.2 collective-permute-done
  296.4 2.9 collective-permute-done.1
  299.4 0.0 collective-permute-done.2
  299.4 3.1 collective-permute-done.3
  302.5 31.4 %fusion.20 = f32[64,180,320]{2,0,1:T(8,128)} fusion(bf16[64,180,320]{2,0,1:T(8,128)(2,1)} %bitcast.26, bf16[1,180,320]{2,0,1:T(2,128)(2,1)S(1)} %collective-permute-done.3, bf16[1,180,320]{2,0,1:T(2,128)(2,1)S(1)} %collective-permute-done.2, bf16[64,1,320]{2,0,1:T(8,128)(2,1)S(1)} %collective-permute-done.1, ...), kind=kLoop, calls=%fused_computation.22 | loop fusion | flops 106905600 | bytes 22432512 | tf_op jit(solution)/shard_map/add | solution.py:109
  (12 shorter events, 0.0 us)
Async XLA Ops:
  12.4 106.8 %all-to-all-start = ((bf16[64,180,320]{2,1,0:T(8,128)(2,1)}), bf16[64,180,320]{2,1,0:T(8,128)(2,1)}, u32[]{:S(2)}, u32[]{:S(2)}) async-start(bf16[64,180,320]{2,1,0:T(8,128)(2,1)} %copy.23), calls=%async_computation | async-start | bytes 18087936 | tf_op jit(solution)/shard_map/all_to_all | solution.py:100
  119.2 8.3 %copy-start.1 = (s32[128]{0:T(128)S(1)}, s32[128]{0:T(128)}, u32[]{:S(2)}) copy-start(s32[128]{0:T(128)} %param.6) | copy-start | bytes 1540
  280.5 21.9 %copy-start = (f32[320]{0:T(512)S(1)}, f32[320]{0:T(512)}, u32[]{:S(2)}) copy-start(f32[320]{0:T(512)} %param.7) | copy-start | bytes 3844
  291.2 8.2 %collective-permute-start.2 = (bf16[1,180,320]{2,0,1:T(2,128)(2,1)S(1)}, bf16[1,180,320]{2,0,1:T(2,128)(2,1)S(1)}, u32[]{:S(2)}, u32[]{:S(2)}) collective-permute-start(bf16[1,180,320]{2,0,1:T(2,128)(2,1)S(1)} %get-tuple-element.137), channel_id=1, source_target_pairs={{0,8},{8,16},{16,24},{1,9},{9,17},{17,25},{2,10},{10,18},{18,26},{... | collective-permute-start | bytes 345608 | tf_op jit(solution)/shard_map/ppermute | solution.py:19
  292.5 9.9 %collective-permute-start.3 = (bf16[1,180,320]{2,0,1:T(2,128)(2,1)S(1)}, bf16[1,180,320]{2,0,1:T(2,128)(2,1)S(1)}, u32[]{:S(2)}, u32[]{:S(2)}) collective-permute-start(bf16[1,180,320]{2,0,1:T(2,128)(2,1)S(1)} %get-tuple-element.138), channel_id=1, source_target_pairs={{8,0},{16,8},{24,16},{9,1},{17,9},{25,17},{10,2},{18,10},{26,18},{... | collective-permute-start | bytes 345608 | tf_op jit(solution)/shard_map/ppermute | solution.py:21
  294.6 1.8 collective-permute-start
  294.7 4.7 %collective-permute-start.1 = (bf16[64,1,320]{2,0,1:T(8,128)(2,1)S(1)}, bf16[64,1,320]{2,0,1:T(8,128)(2,1)S(1)}, u32[]{:S(2)}, u32[]{:S(2)}) collective-permute-start(bf16[64,1,320]{2,0,1:T(8,128)(2,1)S(1)} %get-tuple-element.136), channel_id=1, source_target_pairs={{0,1},{1,2},{2,3},{3,4},{4,5},{5,6},{6,7},{7,0},{8,9},{9,10},{10,1... | collective-permute-start | bytes 122888 | tf_op jit(solution)/shard_map/ppermute | solution.py:19
where the time goes:
time: 336 us; the launch traced here: 334 us
  blocking collectives  105 us (31%)
  other arithmetic  70.5 us (21%)
  waiting for transfers between devices  70 us (21%)
  local copies, waits for them, and re-layouts  44.3 us (13%)
  matrix products  35.6 us (11%)
  starting transfers between devices  8.32 us (2%)
    all_to_all x1, blocking collectives, per_device(): lax.all_to_all(full_rows, 'lon', split_axis=1, concat_axis=0, tiled=True)  105 us
    all_to_all x1, waiting for transfers between devices, per_device(): lax.all_to_all(state, 'lon', split_axis=0, concat_axis=1, tiled=True)  62.9 us
    convert_element_type x1, other arithmetic, fourier_table(): return (fourier.astype(jnp.bfloat16), wavenumber, weights)  38.7 us
    dot_general x1, matrix products, filter_block(): jnp.einsum('jk,rkc->rjc', fourier, damped, preferred_element_type=jnp.flo...  35.6 us
    add x1, other arithmetic, per_device(): updated + viscous * (north_ratio[:, None, None] * (north_q - fields) - so...  31.4 us
    unnamed x5, local copies, waits for them, and re-layouts  12.4 us
    cond x1, local copies, waits for them, and re-layouts, per_device(): full_rows = lax.cond(is_polar, polar_branch, plain_branch, full_rows)  12.1 us
    all_to_all x1, local copies, waits for them, and re-layouts, per_device(): lax.all_to_all(full_rows, 'lon', split_axis=1, concat_axis=0, tiled=True)  8.66 us
  transfers between devices with their start and end apart: 5, of which 4 were waited for; matrix products, arithmetic and copies ran while one was open for 12% of the time, Pallas kernels for 0%

commit v1 on v0

v1 whole, which is shorter than its diff:
```python
import functools
import math

import jax
import jax.numpy as jnp
import ml_dtypes
import numpy as np
from jax import lax
from jax.experimental import pallas as pl
from jax.experimental.pallas import tpu as pltpu
from jax.sharding import PartitionSpec as P

NLON = 1440
MAIN = 256
TAIL = 64
BF = jnp.bfloat16
F32 = jnp.float32
ANY = pl.BlockSpec(memory_space=pl.ANY)
IN_SMEM = pl.BlockSpec(memory_space=pltpu.SMEM)
IN_VMEM = pl.BlockSpec(memory_space=pltpu.VMEM)


def table_pair(count, cols, pad, parity):
    half = NLON // 2
    turns = np.arange(NLON, dtype=np.float32) * np.float32(2.0 * math.pi / NLON)
    cos, sin = np.cos(turns).astype(np.float32), np.sin(turns).astype(np.float32)
    even = np.arange(parity, half + 1, 2)
    odd = even[(even > 0) & (even < half)]
    modes = np.concatenate([even, odd])
    is_cos = np.arange(modes.size) < even.size

    def rows(extra):
        place, live = [], []
        for block in range(count // 2):
            base = block * cols - extra
            used = cols + 2 * extra
            place += [base + i for i in range(used)] + [0] * (pad - used)
            live += [1] * used + [0] * (pad - used)
        turn = (np.array(place)[:, None] % NLON) * modes[None, :] % NLON
        return np.where(is_cos[None, :], cos[turn], sin[turn]) * np.array(live, np.float32)[:, None]

    forward = np.ascontiguousarray(rows(0).T).astype(ml_dtypes.bfloat16)
    return forward, rows(1).astype(ml_dtypes.bfloat16)


def copies(pairs, sems, base=0):
    made = [pltpu.make_async_copy(a, b, sems.at[base + i]) for i, (a, b) in enumerate(pairs)]
    for c in made:
        c.start()
    return made


def wait_all(made):
    for c in made:
        c.wait()


def pack_kernel(cols, pad, count, sets, s, *refs):
    me = s[0]
    n = len(sets)
    x, outs, (raw, work, in_sem, out_sem) = refs[0], refs[1 : 1 + 2 * n], refs[1 + 2 * n :]
    kinds = [(u, i, kind, q) for u, units in enumerate(sets) for i, (kind, q) in enumerate(units)]
    spots, at = [], 0
    for _, _, kind, q in kinds:
        size = count if kind == "main" else 4 * count
        spots.append((q * size, at, size))
        at += size
    loads = copies([(x.at[:, pl.ds(src, size), :], raw.at[:, pl.ds(dst, size), :]) for src, dst, size in spots], in_sem)
    stores = []
    for k, (u, i, kind, _) in enumerate(kinds):
        loads[k].wait()
        dst = spots[k][1]
        if kind == "main":
            flat = raw[:, dst : dst + count, :MAIN]
        else:
            flat = jnp.concatenate(
                [raw[:, dst + t * count : dst + (t + 1) * count, MAIN : MAIN + TAIL] for t in range(4)], axis=-1
            )
        turned = jnp.swapaxes(flat, 0, 1)
        for d in range(count):
            work[k, d, :cols] = turned[d]
            work[k, d, cols:] = jnp.zeros((pad - cols, MAIN), BF)
        lanes = pl.ds(i * MAIN, MAIN)
        pairs = []
        for m in range(count // 2):
            pairs.append((work.at[k, jnp.bitwise_xor(me, 2 * m)], outs[2 * u].at[m, :, lanes]))
            pairs.append((work.at[k, jnp.bitwise_xor(me, 2 * m + 1)], outs[2 * u + 1].at[m, :, lanes]))
        stores += copies(pairs, out_sem, k * count)
    wait_all(stores)


def select_kernel(groups, s, *refs):
    ins, ys, (held, in_sem, out_sem) = refs[: -groups - 3], refs[-groups - 3 : -3], refs[-3:]

    def move(own, par):
        spots = [(m, k) for m in range(groups) for k in range(2)]
        loads = copies([((own, par)[k].at[m], held.at[m, k]) for m, k in spots], in_sem)
        stores = []
        for m in range(groups):
            loads[2 * m].wait()
            loads[2 * m + 1].wait()
            stores += copies([(held.at[m], ys[m])], out_sem, m)
        wait_all(stores)

    if len(ins) == 2:
        move(*ins)
        return

    @pl.when(s[1] == 1)
    def _():
        move(*ins[:2])

    @pl.when(s[1] != 1)
    def _():
        move(*ins[2:])


def filter_kernel(groups, s, cut, *refs):
    me = s[0]
    ins, tables, zs = refs[:groups], refs[groups : groups + 4], refs[groups + 4 : 2 * groups + 4]
    work, done, held, in_sem, table_sem, out_sem = refs[2 * groups + 4 :][0:2] + (refs[2 * groups + 6 : -3],) + refs[-3:]
    count, pad, lanes = work.shape
    half = count // 2
    pairs = []
    for m in range(groups):
        for k in range(2):
            pairs.append((ins[m].at[k], work.at[jnp.bitwise_xor(me, 2 * m + k)]))
    loads = copies(pairs, in_sem)
    table_loads = copies(list(zip(tables, held)), table_sem)
    wait_all(loads)
    low = work[:half].astype(F32)
    high = work[half:].astype(F32)
    cutoff = cut[...]

    def side(values, parity):
        values = values.reshape(half * pad, lanes).astype(BF)
        table_loads[2 * parity].wait()
        forward = held[2 * parity]
        spectrum = jnp.dot(forward[...], values, preferred_element_type=F32)
        index = lax.broadcasted_iota(jnp.int32, (forward.shape[0], 1), 0)
        cosines = NLON // 4 + 1 - parity
        mode = jnp.where(index < cosines, 2 * index + parity, 2 * (index - cosines) + 2 - parity)
        weight = jnp.where((mode == 0) | (mode == NLON // 2), F32(1.0 / NLON), F32(2.0 / NLON))
        damped = (spectrum * jnp.where(mode <= cutoff, weight, F32(0.0))).astype(BF)
        table_loads[2 * parity + 1].wait()
        return jnp.dot(held[2 * parity + 1][...], damped, preferred_element_type=F32)

    even = side(low + high, 0)
    odd = side(low - high, 1)
    done[:half] = (even + odd).reshape(half, pad, lanes).astype(BF)
    done[half:] = (even - odd).reshape(half, pad, lanes).astype(BF)
    pairs = []
    for m in range(groups):
        for k in range(2):
            pairs.append((done.at[jnp.bitwise_xor(me, 2 * m + k)], zs[m].at[k]))
    wait_all(copies(pairs, out_sem))


def gather_kernel(groups, s, *refs):
    ins, outs, (held, in_sem, out_sem) = refs[:groups], refs[groups : groups + 2], refs[groups + 2 :]
    loads = copies([(ins[m], held.at[m]) for m in range(groups)], in_sem)
    stores = []
    for m in range(groups):
        loads[m].wait()
        stores += copies([(held.at[m, k], outs[k].at[m]) for k in range(2)], out_sem, 2 * m)
    wait_all(stores)


def row_of(own, par, rel):
    spot = lax.shift_right_logical(rel, 1)
    return jnp.where(jnp.bitwise_and(rel, 1) == 0, own[spot], par[spot])


def edge_kernel(cols, s, fo, fp, lo, lp, fto, ftp, lto, ltp, x_first, x_last, out_first, out_last):
    me, polar = s[0], s[1]
    count = x_first.shape[1]

    @pl.when(polar == 1)
    def _():
        for spot, own, par, tail_own, tail_par, at, out in (
            (0, fo, fp, fto, ftp, 0, out_first),
            (count - 1, lo, lp, lto, ltp, MAIN - TAIL, out_last),
        ):
            rel = jnp.bitwise_xor(me, spot)
            out[...] = jnp.concatenate(
                [row_of(own, par, rel), row_of(tail_own, tail_par, rel)[:, at : at + TAIL]], axis=-1
            )[1 : cols + 1]

    @pl.when(polar != 1)
    def _():
        out_first[...] = x_first[:, 0, :]
        out_last[...] = x_last[:, count - 1, :]


def final_kernel(cols, count, tiles, places, s, north, south, sides, coef, *refs):
    tails = tiles // 4
    parts, (x, out) = refs[:-11], refs[-11:-9]
    block, tail, own_rows, field, result, block_sem, tail_sem, row_sem, out_sem = refs[-9:]
    me, polar = s[0], s[1]
    width = 15
    groups = count // 2

    def sources(unit, place):
        number, i = places[unit]
        lanes = pl.ds(i * MAIN, MAIN)
        pairs = []
        for m in range(groups):
            for k in range(2):
                pairs.append((parts[2 * number + k].at[m, :, lanes], place(jnp.bitwise_xor(me, 2 * m + k))))
        return pairs

    def main_copies(q):
        slot = q % 2
        pairs = sources(("main", q), lambda d: block.at[slot, d])
        return [pltpu.make_async_copy(a, b, block_sem.at[slot, i]) for i, (a, b) in enumerate(pairs)]

    def tail_copies(t):
        pairs = sources(("tail", t), lambda d: tail.at[t, d])
        return [pltpu.make_async_copy(a, b, tail_sem.at[t, i]) for i, (a, b) in enumerate(pairs)]

    def row_copy(q):
        slot = q % 2
        return pltpu.make_async_copy(x.at[:, pl.ds(q * count, count), :], own_rows.at[slot], row_sem.at[slot])

    def load(q):
        @pl.when(polar == 1)
        def _():
            for c in main_copies(q):
                c.start()

        @pl.when(polar != 1)
        def _():
            row_copy(q).start()

    def prepare(q):
        place = q % 3

        @pl.when(polar == 1)
        def _():
            wait_all(main_copies(q))
            if q % 4 == 0:
                wait_all(tail_copies(q // 4))
            at = q % 4 * TAIL
            rows = jnp.concatenate([block[q % 2], tail[q // 4, :, :, at : at + TAIL]], axis=-1)
            field[place] = jnp.swapaxes(rows, 0, 1)[: cols + 2]

        @pl.when(polar != 1)
        def _():
            row_copy(q).wait()
            field[place, 1 : cols + 1] = own_rows[q % 2]
            field[place, :1] = sides[:1, q * count : (q + 1) * count]
            field[place, cols + 1 :] = sides[1:, q * count : (q + 1) * count]

    def store(q):
        return pltpu.make_async_copy(result.at[q % 2], out.at[:, pl.ds(q * count, count), :], out_sem.at[q % 2])

    @pl.when(polar == 1)
    def _():
        for t in range(tails):
            for c in tail_copies(t):
                c.start()

    load(0)
    load(1)
    prepare(0)
    spot = lax.broadcasted_iota(jnp.int32, (1, count, 1), 1)
    for q in range(tiles):
        if q + 2 < tiles:
            load(q + 2)
        if q + 1 < tiles:
            prepare(q + 1)
        if q >= 2:
            store(q - 2).wait()
        rows = slice(q * count, (q + 1) * count)
        k0, k1, k2, k3 = (coef[i, rows][None] for i in range(4))

        def step(i, carry):
            j = i * width
            f = field[q % 3, pl.ds(j, width + 2)].astype(F32)
            west, here, east = f[:-2], f[1:-1], f[2:]
            if q == 0:
                above = north[pl.ds(j, width)].astype(F32)
            else:
                above = field[(q - 1) % 3, pl.ds(j + 1, width)].astype(F32)
            if q == tiles - 1:
                below = south[pl.ds(j, width)].astype(F32)
            else:
                below = field[(q + 1) % 3, pl.ds(j + 1, width)].astype(F32)
            up = pltpu.roll(jnp.where(spot == count - 1, above, here), 1, 1)
            down = pltpu.roll(jnp.where(spot == 0, below, here), count - 1, 1)
            result[q % 2, pl.ds(j, width)] = k0 * here + k1 * (west + east) + (k2 * up + k3 * down)
            return carry

        lax.fori_loop(0, cols // width, step, 0)
        store(q).start()
    for q in range(max(tiles - 2, 0), tiles):
        store(q).wait()


def metric(global_rows, nlat):
    spacing = jnp.float32(math.pi / nlat)
    rows_f = global_rows.astype(jnp.float32)
    cell_cos = jnp.sin((rows_f + 0.5) * spacing)
    north_cos = jnp.where(global_rows == 0, jnp.float32(0.0), jnp.sin(rows_f * spacing))
    south_cos = jnp.where(global_rows == nlat - 1, jnp.float32(0.0), jnp.sin((rows_f + 1.0) * spacing))
    return (north_cos / cell_cos, south_cos / cell_cos)


def per_device(state, cutoff, viscosity):
    rows, cols, channels = state.shape
    lats = lax.axis_size("lat")
    count = lax.axis_size("lon")
    groups = count // 2
    nlat = rows * lats
    pad = -(-(cols + 2) // 8) * 8
    tiles = rows // count
    tails = tiles // 4
    lat, me = lax.axis_index("lat"), lax.axis_index("lon")
    edge = lats // 4
    is_polar = (lat < edge) | (lat >= lats - edge)
    flags = jnp.stack([me, is_polar.astype(jnp.int32)]).astype(jnp.int32)
    x = jnp.transpose(state, (1, 0, 2))

    helpers = [(i, i + edge) for i in range(edge)] + [(lats - 1 - i, lats - 1 - i - edge) for i in range(edge)]

    served = jnp.where(is_polar, lat, jnp.where(lat < lats // 2, lat - edge, lat + edge))
    served = jnp.where(served < lats // 2, served, served - lats // 2)
    cut_rows = lax.dynamic_slice_in_dim(cutoff, served * rows, rows)
    cut_mine = jnp.sum(
        jnp.where(jnp.arange(count)[None, :] == me, cut_rows.reshape(tiles, count), 0), axis=1
    )

    tables = []
    for parity in (0, 1):
        tables += [jnp.asarray(t) for t in table_pair(count, cols, pad, parity)]

    def block(n_blocks, lanes):
        return jax.ShapeDtypeStruct((n_blocks, pad, lanes), BF)

    def tie(value, *others):
        return lax.optimization_barrier((value, *others))[0] if others else value

    ran = []

    def call(kernel, arrays, specs, outs, name, scratch, after=(), out_specs=None):
        results = pl.pallas_call(
            kernel,
            in_specs=[IN_SMEM] + specs,
            out_specs=out_specs or [ANY] * len(outs),
            out_shape=outs,
            scratch_shapes=scratch,
            compiler_params=pltpu.CompilerParams(vmem_limit_bytes=60 * 2**20),
            cost_estimate=pl.CostEstimate(flops=1, bytes_accessed=1, transcendentals=0),
            name=name,
        )(tie(flags, *ran[-1:], *after), *arrays)
        ran.append(results[0])
        return results

    def sems(*shape):
        return pltpu.SemaphoreType.DMA(shape)

    def swapped(value):
        return lax.ppermute(value, "lon", [(i, i ^ 1) for i in range(count)])

    def pack(sets):
        units = [unit for group in sets for unit in group]
        size = sum(count if kind == "main" else 4 * count for kind, _ in units)
        shapes = [block(groups, MAIN * len(group)) for group in sets for _ in range(2)]
        outs = call(
            functools.partial(pack_kernel, cols, pad, count, sets), [x], [ANY], shapes, "pack",
            [
                pltpu.VMEM((cols, size, channels), BF), pltpu.VMEM((len(units), count, pad, MAIN), BF),
                sems(len(units)), sems(len(units) * count),
            ],
        )
        return [(outs[2 * u], outs[2 * u + 1]) for u in range(len(sets))]

    def hop(own, par, pairs):
        crossed = [(a * count + i, b * count + (i ^ 1)) for a, b in pairs for i in range(count)]
        return (lax.ppermute(own, "lat", pairs), lax.ppermute(par, ("lat", "lon"), crossed))

    def select(own, lifted=(), after=()):
        arrays = [*own, *lifted]
        lanes = own[0].shape[-1]
        return call(
            functools.partial(select_kernel, groups), arrays, [ANY] * len(arrays), [block(2, lanes)] * groups, "select",
            [pltpu.VMEM((groups, 2, pad, lanes), BF), sems(count), sems(groups)], after,
        )

    def cut_of(own_units, helped_units):
        def lanes_of(units):
            parts = []
            for kind, q in units:
                if kind == "main":
                    parts.append(jnp.broadcast_to(cut_mine[q], (MAIN,)))
                else:
                    parts.append(jnp.repeat(cut_mine[4 * q : 4 * q + 4], TAIL))
            return jnp.concatenate(parts)[None, :]

        own = lanes_of(own_units)
        return jnp.where(is_polar, own, lanes_of(helped_units)) if helped_units else own

    def run_filter(pieces, cut):
        lanes = cut.shape[-1]
        return call(
            functools.partial(filter_kernel, groups), [cut, *pieces, *tables], [IN_VMEM] + [ANY] * (groups + 4),
            [block(2, lanes)] * groups, "filter",
            [pltpu.VMEM((count, pad, lanes), BF)] * 2 + [pltpu.VMEM(t.shape, BF) for t in tables]
            + [sems(count), sems(4), sems(count)],
        )

    sent = []

    def exchange(pieces):
        got = [pieces[0]]
        for m in range(1, groups):
            value = tie(pieces[m], *(sent[1 - groups :][:1] if len(sent) >= groups - 1 else ()))
            sent.append(lax.ppermute(value, "lon", [(i, i ^ (2 * m)) for i in range(count)]))
            got.append(sent[-1])
        return got

    def gather(pieces):
        lanes = pieces[0].shape[-1]
        return call(
            functools.partial(gather_kernel, groups), pieces, [ANY] * groups, [block(groups, lanes)] * 2, "gather",
            [pltpu.VMEM((groups, 2, pad, lanes), BF), sems(groups), sems(count)],
        )

    mains = [("main", q) for q in range(tiles)]
    tail_units = [("tail", t) for t in range(tails)]
    order = [mains[tiles - 1], mains[0]] + mains[1 : tiles - 1]
    big = (tiles + tails) // 5
    helped = [order[:big], order[big : big + 1]]
    others = tail_units + order[big + 1 :]
    shared = [others[:big], others[big : big + 1]]
    lone = [others[i : i + big] for i in range(big + 1, len(others), big)]

    sides = jnp.concatenate(
        [
            lax.ppermute(x[cols - 1 :], "lon", [(i, (i + 1) % count) for i in range(count)]),
            lax.ppermute(x[:1], "lon", [((i + 1) % count, i) for i in range(count)]),
        ],
        axis=0,
    )

    back = [(b, a) for a, b in helpers]
    done, places = [], {}

    def finish(units, pair):
        for i, unit in enumerate(units):
            places[unit] = (len(done) // 2, i)
        done.extend(pair)

    def give(units, zs, helped_units=()):
        own, par = gather(zs)
        finish(units, (own, swapped(par)))
        if helped_units:
            finish(helped_units, hop(own, par, back))

    def apart(pair):
        return (pair[0], swapped(pair[1]))

    first_helped, first_lone = pack([helped[0], lone[0]])
    lifted = [hop(*first_helped, helpers)]
    got_lone = [exchange(select(apart(first_lone)))]
    later = pack(lone[1:] + shared + helped[1:])
    more_lone, own = later[: len(lone) - 1], later[len(lone) - 1 : len(lone) + 1]
    own = [apart(pair) for pair in own]
    more_lone = [apart(pair) for pair in more_lone]
    for pair in more_lone:
        got_lone.append(exchange(select(pair)))
    ys = select(own[0], lifted[0])
    lifted.append(hop(*(tie(v, ys[0]) for v in later[-1]), helpers))
    got = exchange(ys)
    z_lone = [run_filter(g, cut_of(units, [])) for g, units in zip(got_lone, lone)]
    zs = exchange(run_filter(got, cut_of(shared[0], helped[0])))
    ys = select(own[1], lifted[1])
    got = exchange(ys)
    give(shared[0], zs, helped[0])
    zs = exchange(run_filter(got, cut_of(shared[1], helped[1])))
    z_lone = [exchange([tie(v, ran[-1]) for v in z]) for z in z_lone]
    give(shared[1], zs, helped[1])
    for z, units in zip(z_lone, lone):
        give(units, z)

    edge_arrays, edge_specs = [], []
    for unit in (mains[0], mains[tiles - 1], tail_units[0], tail_units[tails - 1]):
        number, i = places[unit]
        edge_arrays += done[2 * number : 2 * number + 2]
        edge_specs += [pl.BlockSpec((groups, pad, MAIN), functools.partial(lambda k, i: (0, 0, k), i))] * 2

    def tile_spec(q):
        return pl.BlockSpec((cols, count, channels), lambda i: (0, q, 0))

    first, last = pl.pallas_call(
        functools.partial(edge_kernel, cols),
        grid=(1,),
        in_specs=[IN_SMEM] + edge_specs + [tile_spec(0), tile_spec(tiles - 1)],
        out_specs=[pl.BlockSpec((cols, channels), lambda i: (0, 0))] * 2,
        out_shape=[jax.ShapeDtypeStruct((cols, channels), BF)] * 2,
        compiler_params=pltpu.CompilerParams(vmem_limit_bytes=60 * 2**20),
        cost_estimate=pl.CostEstimate(flops=1, bytes_accessed=1, transcendentals=0),
        name="edges",
    )(flags, *edge_arrays, x, x)
    north = lax.ppermute(last, "lat", [(i, i + 1) for i in range(lats - 1)]).reshape(cols, 1, channels)
    south = lax.ppermute(first, "lat", [(i + 1, i) for i in range(lats - 1)]).reshape(cols, 1, channels)

    tile_rows = lat * rows + jnp.arange(rows, dtype=jnp.int32)
    north_ratio, south_ratio = metric(tile_rows, nlat)
    v = jnp.broadcast_to(viscosity[None, :], (rows, channels))
    a, b = north_ratio[:, None] * v, south_ratio[:, None] * v
    coef = jnp.stack([1.0 - 2.0 * v - a - b, v, a, b])

    updated = call(
        functools.partial(final_kernel, cols, count, tiles, places),
        [north, south, sides, coef, *done, x],
        [IN_VMEM] * 4 + [ANY] * (len(done) + 1),
        [jax.ShapeDtypeStruct((cols, rows, channels), F32)], "flux_step",
        [
            pltpu.VMEM((2, count, pad, MAIN), BF), pltpu.VMEM((tails, count, pad, MAIN), BF),
            pltpu.VMEM((2, cols, count, channels), BF), pltpu.VMEM((3, cols + 2, count, channels), BF),
            pltpu.VMEM((2, cols, count, channels), F32),
            sems(2, count), sems(tails, count), sems(2), sems(2),
        ],
    )[0]
    return jnp.transpose(updated, (1, 0, 2))


def solution(mesh):
    in_specs = (P("lat", "lon", None), P(), P())
    out_specs = P("lat", "lon", None)
    return jax.shard_map(per_device, mesh=mesh, in_specs=in_specs, out_specs=out_specs, check_vma=False)
```

time: 336 us -> 249 us (0.74)
  blocking collectives: 105 us -> 0 us
  Pallas kernels: 0 us -> 88.1 us
  other arithmetic: 70.5 us -> 3.6 us
  starting transfers between devices: 8.32 us -> 52 us
  matrix products: 35.6 us -> 0 us
  local copies, waits for them, and re-layouts: 44.3 us -> 15.6 us
  waiting for transfers between devices: 70 us -> 86.2 us
    all_to_all x1 -> x0, blocking collectives: 105 us -> none  [per_device(): lax.all_to_all(full_rows, 'lon', split_axis=1, concat_axis=0, tiled=True)]
    pallas_call x0 -> x16, Pallas kernels: none -> 88.1 us  [the longest x15 84.7 us: call(): pl.pallas_call(kernel, in_specs=[IN_SMEM] + specs, out_specs=out_specs or...]
    ppermute x4 -> x44, waiting for transfers between devices: 7.18 us -> 86.2 us  [the longest x24 58.7 us: exchange(): lax.ppermute(value, 'lon', [(i, i ^ 2 * m) for i in range(count)])]
    all_to_all x1 -> x0, waiting for transfers between devices: 62.9 us -> none  [per_device(): lax.all_to_all(state, 'lon', split_axis=0, concat_axis=1, tiled=True)]
    ppermute x4 -> x44, starting transfers between devices: 3.15 us -> 52 us  [the longest x24 30.7 us: exchange(): lax.ppermute(value, 'lon', [(i, i ^ 2 * m) for i in range(count)])]
    convert_element_type x1 -> x0, other arithmetic: 38.7 us -> none  [fourier_table(): return (fourier.astype(jnp.bfloat16), wavenumber, weights)]
    dot_general x1 -> x0, matrix products: 35.6 us -> none  [filter_block(): jnp.einsum('jk,rkc->rjc', fourier, damped, preferred_element_type=jnp.flo...]
    add x1 -> x0, other arithmetic: 31.4 us -> none  [per_device(): updated + viscous * (north_ratio[:, None, None] * (north_q - fields) - so...]
  transfers between devices with their start and end apart: 5 -> 44, of which waited for: 4 -> 18; matrix products, arithmetic and copies ran while one was open for 12% -> 4% of each run, Pallas kernels for 0% -> 19%
where the time goes in v1:
time: 249 us; the launch traced here: 248 us
  Pallas kernels  88.1 us (35%)
  waiting for transfers between devices  86.2 us (35%)
  starting transfers between devices  52 us (21%)
  local copies, waits for them, and re-layouts  15.6 us (6%)
  other arithmetic  3.6 us (1%)
    pallas_call x15, Pallas kernels, call(): pl.pallas_call(kernel, in_specs=[IN_SMEM] + specs, out_specs=out_specs or...  84.7 us
    ppermute x24, waiting for transfers between devices, exchange(): lax.ppermute(value, 'lon', [(i, i ^ 2 * m) for i in range(count)])  58.7 us
    ppermute x24, starting transfers between devices, exchange(): lax.ppermute(value, 'lon', [(i, i ^ 2 * m) for i in range(count)])  30.7 us
    ppermute x4, waiting for transfers between devices, hop(): lax.ppermute(own, 'lat', pairs)  17.1 us
    ppermute x4, starting transfers between devices, hop(): lax.ppermute(par, ('lat', 'lon'), crossed)  7.25 us
    unnamed x84, local copies, waits for them, and re-layouts  6.83 us
    ppermute x4, waiting for transfers between devices, hop(): lax.ppermute(par, ('lat', 'lon'), crossed)  6.67 us
    ppermute x4, starting transfers between devices, hop(): lax.ppermute(own, 'lat', pairs)  5.97 us
  transfers between devices with their start and end apart: 44, of which 18 were waited for; matrix products, arithmetic and copies ran while one was open for 4% of the time, Pallas kernels for 19%

profile of v1, /device:TPU:0, one launch (start us, length us, event | category | flops | bytes accessed | tf_op | source)
XLA Modules:
  0.0 247.6 jit_solution(2253437924499348695)
XLA Ops:
  0.6 4.3 %pack.2 = (bf16[4,184,512]{2,1,0:T(8,128)(2,1)}, bf16[4,184,512]{2,1,0:T(8,128)(2,1)}, bf16[4,184,512]{2,1,0:T(8,128)(2,1)}, bf16[4,184,512]{2,1,0:T(8,128)(2,1)}) custom-call(s32[2]{0:T(128)} %pad_add_fusion.s, bf16[180,64,320]{2,1,0:T(8,128)(2,1)} %bitcast.17), custom_call_target="tpu_custom_call" | custom-call | flops 1 | bytes 1 | tf_op jit(solution)/shard_map/pack/pallas_call | solution.py:346
  8.4 3.0 %select.7 = (bf16[2,184,512]{2,1,0:T(8,128)(2,1)}, bf16[2,184,512]{2,1,0:T(8,128)(2,1)}, bf16[2,184,512]{2,1,0:T(8,128)(2,1)}, bf16[2,184,512]{2,1,0:T(8,128)(2,1)}) custom-call(s32[2]{0:T(128)} %pad_add_fusion.s, bf16[4,184,512]{2,1,0:T(8,128)(2,1)} %get-tuple-element.106.refs_0_, bf16[4,184,512]{2,1,0:T(8,128)(2,1)} %copy-done.8), custom_call_target="tpu_custom_call" | custom-call | flops 1 | bytes 1 | tf_op jit(solution)/shard_map/select/pallas_call | solution.py:346
  11.4 8.0 %pack.3 = (bf16[4,184,512]{2,1,0:T(8,128)(2,1)}, bf16[4,184,512]{2,1,0:T(8,128)(2,1)}, bf16[4,184,512]{2,1,0:T(8,128)(2,1)}, bf16[4,184,512]{2,1,0:T(8,128)(2,1)...) custom-call(s32[2]{0:T(128)} %pad_add_fusion.s, ...), custom_call_target="tpu_custom_call" | custom-call | flops 1 | bytes 1 | tf_op jit(solution)/shard_map/pack/pallas_call | solution.py:346
  22.5 3.2 %collective-permute-start.4 = (bf16[4,184,512]{2,1,0:T(8,128)(2,1)}, bf16[4,184,512]{2,1,0:T(8,128)(2,1)S(1)}, u32[]{:S(2)}, u32[]{:S(2)}) collective-permute-start(bf16[4,184,512]{2,1,0:T(8,128)(2,1)} %get-tuple-element.117), channel_id=1, source_target_pairs={{0,9},{1,8},{2,11},{3,10},{4,13},{5,12},{6,15},{7,14},{24,17},{25,... | collective-permute-start | bytes 2261000 | tf_op jit(solution)/shard_map/ppermute | solution.py:380
  34.5 3.0 %select.8 = (bf16[2,184,512]{2,1,0:T(8,128)(2,1)}, bf16[2,184,512]{2,1,0:T(8,128)(2,1)}, bf16[2,184,512]{2,1,0:T(8,128)(2,1)}, bf16[2,184,512]{2,1,0:T(8,128)(2,1)}) custom-call(s32[2]{0:T(128)} %pad_add_fusion.s, bf16[4,184,512]{2,1,0:T(8,128)(2,1)} %get-tuple-element.110.refs_0_, bf16[4,184,512]{2,1,0:T(8,128)(2,1)} %copy-done.7), custom_call_target="tpu_custom_call" | custom-call | flops 1 | bytes 1 | tf_op jit(solution)/shard_map/select/pallas_call | solution.py:346
  37.5 9.0 %collective-permute-done.6.refs_2_ = bf16[2,184,512]{2,1,0:T(8,128)(2,1)S(1)} collective-permute-done((bf16[2,184,512]{2,1,0:T(8,128)(2,1)}, bf16[2,184,512]{2,1,0:T(8,128)(2,1)S(1)}, u32[]{:S(2)}, u32[]{:S(2)}) %collective-permute-start.6) | collective-permute-done | bytes 376864 | tf_op jit(solution)/shard_map/ppermute | solution.py:418
  50.3 8.7 %collective-permute-done.3.refs_2_ = bf16[4,184,512]{2,1,0:T(8,128)(2,1)S(1)} collective-permute-done((bf16[4,184,512]{2,1,0:T(8,128)(2,1)}, bf16[4,184,512]{2,1,0:T(8,128)(2,1)S(1)}, u32[]{:S(2)}, u32[]{:S(2)}) %collective-permute-start.3) | collective-permute-done | bytes 753696 | tf_op jit(solution)/shard_map/ppermute | solution.py:380
  60.2 3.0 %select.9 = (bf16[2,184,512]{2,1,0:T(8,128)(2,1)}, bf16[2,184,512]{2,1,0:T(8,128)(2,1)}, bf16[2,184,512]{2,1,0:T(8,128)(2,1)}, bf16[2,184,512]{2,1,0:T(8,128)(2,1)}) custom-call(s32[2]{0:T(128)} %pad_add_fusion.s, bf16[4,184,512]{2,1,0:T(8,128)(2,1)} %get-tuple-element.115.refs_0_, bf16[4,184,512]{2,1,0:T(8,128)(2,1)} %copy-done.6, ...), custom_call_target="tpu_custom_call" | custom-call | flops 1 | bytes 1 | tf_op jit(solution)/shard_map/select/pallas_call | solution.py:346
  75.8 8.0 %filter.4 = (bf16[2,184,512]{2,1,0:T(8,128)(2,1)}, bf16[2,184,512]{2,1,0:T(8,128)(2,1)}, bf16[2,184,512]{2,1,0:T(8,128)(2,1)}, bf16[2,184,512]{2,1,0:T(8,128)(2,1)}) custom-call(s32[2]{0:T(128)} %pad_add_fusion.s, s32[1,512]{1,0:T(1,128)} %bitcast.27, bf16[2,184,512]{2,1,0:T(8,128)(2,1)} %get-tuple-element.108.refs_0_, bf16[2,184,512]{2,1,0:T(8,128)(2,1)} %copy-done.15, ...), custom_call_target="tpu_custom_call" | custom-call | flops 1 | bytes 1 | tf_op jit(solution)/shard_map/filter/pallas_call | solution.py:346
  85.6 8.0 %filter.5 = (bf16[2,184,512]{2,1,0:T(8,128)(2,1)}, bf16[2,184,512]{2,1,0:T(8,128)(2,1)}, bf16[2,184,512]{2,1,0:T(8,128)(2,1)}, bf16[2,184,512]{2,1,0:T(8,128)(2,1)}) custom-call(s32[2]{0:T(128)} %pad_add_fusion.s, s32[1,512]{1,0:T(1,128)} %bitcast.26, bf16[2,184,512]{2,1,0:T(8,128)(2,1)} %get-tuple-element.113.refs_0_, bf16[2,184,512]{2,1,0:T(8,128)(2,1)} %copy-done.17, ...), custom_call_target="tpu_custom_call" | custom-call | flops 1 | bytes 1 | tf_op jit(solution)/shard_map/filter/pallas_call | solution.py:346
  96.1 7.8 %filter.6 = (bf16[2,184,512]{2,1,0:T(8,128)(2,1)}, bf16[2,184,512]{2,1,0:T(8,128)(2,1)}, bf16[2,184,512]{2,1,0:T(8,128)(2,1)}, bf16[2,184,512]{2,1,0:T(8,128)(2,1)}) custom-call(s32[2]{0:T(128)} %pad_add_fusion.s, s32[1,512]{1,0:T(1,128)} %bitcast.25, bf16[2,184,512]{2,1,0:T(8,128)(2,1)} %get-tuple-element.118.refs_0_, bf16[2,184,512]{2,1,0:T(8,128)(2,1)} %copy-done.21, ...), custom_call_target="tpu_custom_call" | custom-call | flops 1 | bytes 1 | tf_op jit(solution)/shard_map/filter/pallas_call | solution.py:346
  111.0 5.7 %collective-permute-done.19.refs_3_ = bf16[2,184,512]{2,1,0:T(8,128)(2,1)S(1)} collective-permute-done((bf16[2,184,512]{2,1,0:T(8,128)(2,1)}, bf16[2,184,512]{2,1,0:T(8,128)(2,1)S(1)}, u32[]{:S(2)}, u32[]{:S(2)}) %collective-permute-start.19) | collective-permute-done | bytes 376864 | tf_op jit(solution)/shard_map/ppermute | solution.py:418
  118.2 6.5 %collective-permute-done.18.refs_2_ = bf16[2,184,512]{2,1,0:T(8,128)(2,1)S(1)} collective-permute-done((bf16[2,184,512]{2,1,0:T(8,128)(2,1)}, bf16[2,184,512]{2,1,0:T(8,128)(2,1)S(1)}, u32[]{:S(2)}, u32[]{:S(2)}) %collective-permute-start.18) | collective-permute-done | bytes 376864 | tf_op jit(solution)/shard_map/ppermute | solution.py:418
  132.8 7.0 %filter.7 = (bf16[2,184,256]{2,1,0:T(8,128)(2,1)}, bf16[2,184,256]{2,1,0:T(8,128)(2,1)}, bf16[2,184,256]{2,1,0:T(8,128)(2,1)}, bf16[2,184,256]{2,1,0:T(8,128)(2,1)}) custom-call(s32[2]{0:T(128)} %pad_add_fusion.s, s32[1,256]{1,0:T(1,128)} %select_n.59.cut, bf16[2,184,256]{2,1,0:T(8,128)(2,1)} %get-tuple-element.147.refs_0_, bf16[2,184,256]{2,1,0:T(8,128)(2,1)} %copy-done.33, ...), custom_call_target="tpu_custom_call" | custom-call | flops 1 | bytes 1 | tf_op jit(solution)/shard_map/filter/pallas_call | solution.py:346
  141.1 5.3 %collective-permute-done.23.refs_1_ = bf16[2,184,256]{2,1,0:T(8,128)(2,1)S(1)} collective-permute-done((bf16[2,184,256]{2,1,0:T(8,128)(2,1)}, bf16[2,184,256]{2,1,0:T(8,128)(2,1)S(1)}, u32[]{:S(2)}, u32[]{:S(2)}) %collective-permute-start.23) | collective-permute-done | bytes 188448 | tf_op jit(solution)/shard_map/ppermute | solution.py:418
  151.1 3.1 %collective-permute-done.24.refs_2_ = bf16[2,184,256]{2,1,0:T(8,128)(2,1)S(1)} collective-permute-done((bf16[2,184,256]{2,1,0:T(8,128)(2,1)}, bf16[2,184,256]{2,1,0:T(8,128)(2,1)S(1)}, u32[]{:S(2)}, u32[]{:S(2)}) %collective-permute-start.24) | collective-permute-done | bytes 188448 | tf_op jit(solution)/shard_map/ppermute | solution.py:418
  155.6 6.4 %collective-permute-done.25.refs_3_ = bf16[2,184,256]{2,1,0:T(8,128)(2,1)} collective-permute-done((bf16[2,184,256]{2,1,0:T(8,128)(2,1)}, bf16[2,184,256]{2,1,0:T(8,128)(2,1)}, u32[]{:S(2)}, u32[]{:S(2)}) %collective-permute-start.25) | collective-permute-done | bytes 188448 | tf_op jit(solution)/shard_map/ppermute | solution.py:418
  163.7 15.3 %collective-permute-done.27.refs_2_ = bf16[2,184,512]{2,1,0:T(8,128)(2,1)S(1)} collective-permute-done((bf16[2,184,512]{2,1,0:T(8,128)(2,1)S(1)}, bf16[2,184,512]{2,1,0:T(8,128)(2,1)S(1)}, u32[]{:S(2)}, u32[]{:S(2)}) %collective-permute-start.27) | collective-permute-done | bytes 376864 | tf_op jit(solution)/shard_map/ppermute | solution.py:418
  186.0 3.0 %gather.6 = (bf16[4,184,512]{2,1,0:T(8,128)(2,1)}, bf16[4,184,512]{2,1,0:T(8,128)(2,1)}) custom-call(s32[2]{0:T(128)} %pad_add_fusion.s, bf16[2,184,512]{2,1,0:T(8,128)(2,1)} %get-tuple-element.173.refs_0_, bf16[2,184,512]{2,1,0:T(8,128)(2,1)} %copy-done.22, bf16[2,184,512]{2,1,0:T(8,128)(2,1)} %copy-done.29, bf16[2,184,512]{2,1,0:T(8,128)(2,1)} %copy-done.30), custom_call_target="tpu_custom_call" | custom-call | flops 1 | bytes 1 | tf_op jit(solution)/shard_map/gather/pallas_call | solution.py:346
  190.2 3.4 %edges.1 = (bf16[180,320]{1,0:T(8,128)(2,1)}, bf16[180,320]{1,0:T(8,128)(2,1)}) custom-call(s32[2]{0:T(128)} %pad_add_fusion.s, bf16[4,184,512]{2,1,0:T(8,128)(2,1)} %copy-done.3, bf16[4,184,512]{2,1,0:T(8,128)(2,1)} %copy-done.2, bf16[4,184,512]{2,1,0:T(8,128)(2,1)} %copy-done.3, bf16[4,184,512]{2,1,0:T(8,128)(2,1)} %copy-done.2, ...), custom_call_target="tpu_custom_call" | custom-call | flops 1 | bytes 1 | tf_op jit(solution)/shard_map/edges/pallas_call | solution.py:495
  193.6 3.0 %collective-permute-start.35 = (bf16[180,320]{1,0:T(8,128)(2,1)}, bf16[180,320]{1,0:T(8,128)(2,1)S(1)}, u32[]{:S(2)}, u32[]{:S(2)}) collective-permute-start(bf16[180,320]{1,0:T(8,128)(2,1)} %get-tuple-element.198), channel_id=1, source_target_pairs={{0,8},{8,16},{16,24},{1,9},{9,17},{17,25},{2,10},{10,18},{18,26},{... | collective-permute-start | bytes 345608 | tf_op jit(solution)/shard_map/ppermute | solution.py:505
  211.8 6.7 %collective-permute-done.41.refs_7_ = bf16[4,184,256]{2,1,0:T(8,128)(2,1)S(1)} collective-permute-done((bf16[4,184,256]{2,1,0:T(8,128)(2,1)}, bf16[4,184,256]{2,1,0:T(8,128)(2,1)S(1)}, u32[]{:S(2)}, u32[]{:S(2)}) %collective-permute-start.41) | collective-permute-done | bytes 376864 | tf_op jit(solution)/shard_map/ppermute | solution.py:380
  218.5 8.4 %collective-permute-done.40.refs_6_ = bf16[4,184,256]{2,1,0:T(8,128)(2,1)S(1)} collective-permute-done((bf16[4,184,256]{2,1,0:T(8,128)(2,1)S(1)}, bf16[4,184,256]{2,1,0:T(8,128)(2,1)S(1)}, u32[]{:S(2)}, u32[]{:S(2)}) %collective-permute-start.40) | collective-permute-done | bytes 376864 | tf_op jit(solution)/shard_map/ppermute | solution.py:380
  228.8 18.6 %flux_step.1 = f32[180,64,320]{2,1,0:T(8,128)} custom-call(s32[2]{0:T(128)} %pad_add_fusion.s, bf16[180,1,320]{2,1,0:T(2,128)(2,1)} %copy.8.north, bf16[180,1,320]{2,1,0:T(2,128)(2,1)} %copy.9.south, bf16[2,64,320]{2,1,0:T(8,128)(2,1)} %pad_maximum_fusion.1.sides, f32[4,64,320]{2,1,0:T(8,128)} %pad_maximum_fusion.coef, ...), custom_call_target="tpu_custom_call" | custom-call | flops 1 | bytes 1 | tf_op jit(solution)/shard_map/flux_step/pallas_call | solution.py:346
  (191 shorter events, 87.3 us)
Async XLA Ops:
  22.5 26.1 %collective-permute-start.4 = (bf16[4,184,512]{2,1,0:T(8,128)(2,1)}, bf16[4,184,512]{2,1,0:T(8,128)(2,1)S(1)}, u32[]{:S(2)}, u32[]{:S(2)}) collective-permute-start(bf16[4,184,512]{2,1,0:T(8,128)(2,1)} %get-tuple-element.117), channel_id=1, source_target_pairs={{0,9},{1,8},{2,11},{3,10},{4,13},{5,12},{6,15},{7,14},{24,17},{25,... | collective-permute-start | bytes 2261000 | tf_op jit(solution)/shard_map/ppermute | solution.py:380
  25.7 33.4 %collective-permute-start.3 = (bf16[4,184,512]{2,1,0:T(8,128)(2,1)}, bf16[4,184,512]{2,1,0:T(8,128)(2,1)S(1)}, u32[]{:S(2)}, u32[]{:S(2)}) collective-permute-start(bf16[4,184,512]{2,1,0:T(8,128)(2,1)} %get-tuple-element.104), channel_id=1, source_target_pairs={{0,8},{24,16},{1,9},{25,17},{2,10},{26,18},{3,11},{27,19},{4,12},{... | collective-permute-start | bytes 2261000 | tf_op jit(solution)/shard_map/ppermute | solution.py:380
  27.3 19.2 %collective-permute-start.6 = (bf16[2,184,512]{2,1,0:T(8,128)(2,1)}, bf16[2,184,512]{2,1,0:T(8,128)(2,1)S(1)}, u32[]{:S(2)}, u32[]{:S(2)}) collective-permute-start(bf16[2,184,512]{2,1,0:T(8,128)(2,1)} %get-tuple-element.121), channel_id=1, source_target_pairs={{0,4},{1,5},{2,6},{3,7},{4,0},{5,1},{6,2},{7,3},{8,12},{9,13},{10,... | collective-permute-start | bytes 1130504 | tf_op jit(solution)/shard_map/ppermute | solution.py:418
  31.8 27.3 %collective-permute-start.2 = (bf16[4,184,512]{2,1,0:T(8,128)(2,1)}, bf16[4,184,512]{2,1,0:T(8,128)(2,1)S(1)}, u32[]{:S(2)}, u32[]{:S(2)}) collective-permute-start(bf16[4,184,512]{2,1,0:T(8,128)(2,1)} %get-tuple-element.116), channel_id=1, source_target_pairs={{0,1},{1,0},{2,3},{3,2},{4,5},{5,4},{6,7},{7,6},{8,9},{9,8},{10,11... | collective-permute-start | bytes 2261000 | tf_op jit(solution)/shard_map/ppermute | solution.py:363
  46.5 16.7 %collective-permute-start.8 = (bf16[2,184,512]{2,1,0:T(8,128)(2,1)}, bf16[2,184,512]{2,1,0:T(8,128)(2,1)S(1)}, u32[]{:S(2)}, u32[]{:S(2)}) collective-permute-start(bf16[2,184,512]{2,1,0:T(8,128)(2,1)} %get-tuple-element.126), channel_id=1, source_target_pairs={{0,2},{1,3},{2,0},{3,1},{4,6},{5,7},{6,4},{7,5},{8,10},{9,11},{10,... | collective-permute-start | bytes 1130504 | tf_op jit(solution)/shard_map/ppermute | solution.py:418
  47.0 17.2 %collective-permute-start.9 = (bf16[2,184,512]{2,1,0:T(8,128)(2,1)}, bf16[2,184,512]{2,1,0:T(8,128)(2,1)}, u32[]{:S(2)}, u32[]{:S(2)}) collective-permute-start(bf16[2,184,512]{2,1,0:T(8,128)(2,1)} %get-tuple-element.128), channel_id=1, source_target_pairs={{0,4},{1,5},{2,6},{3,7},{4,0},{5,1},{6,2},{7,3},{8,12},{9,13},{10,... | collective-permute-start | bytes 1130504 | tf_op jit(solution)/shard_map/ppermute | solution.py:418
  48.5 17.3 %collective-permute-start.10 = (bf16[2,184,512]{2,1,0:T(8,128)(2,1)}, bf16[2,184,512]{2,1,0:T(8,128)(2,1)}, u32[]{:S(2)}, u32[]{:S(2)}) collective-permute-start(bf16[2,184,512]{2,1,0:T(8,128)(2,1)} %get-tuple-element.130), channel_id=1, source_target_pairs={{0,6},{1,7},{2,4},{3,5},{4,2},{5,3},{6,0},{7,1},{8,14},{9,15},{10,... | collective-permute-start | bytes 1130504 | tf_op jit(solution)/shard_map/ppermute | solution.py:418
  59.1 46.9 %collective-permute-start.14 = (bf16[4,184,256]{2,1,0:T(8,128)(2,1)}, bf16[4,184,256]{2,1,0:T(8,128)(2,1)S(1)}, u32[]{:S(2)}, u32[]{:S(2)}) collective-permute-start(bf16[4,184,256]{2,1,0:T(8,128)(2,1)} %get-tuple-element.142), channel_id=1, source_target_pairs={{0,1},{1,0},{2,3},{3,2},{4,5},{5,4},{6,7},{7,6},{8,9},{9,8},{10,11... | collective-permute-start | bytes 1130504 | tf_op jit(solution)/shard_map/ppermute | solution.py:363
  65.8 27.8 %collective-permute-start.13 = (bf16[2,184,512]{2,1,0:T(8,128)(2,1)}, bf16[2,184,512]{2,1,0:T(8,128)(2,1)S(1)}, u32[]{:S(2)}, u32[]{:S(2)}) collective-permute-start(bf16[2,184,512]{2,1,0:T(8,128)(2,1)} %get-tuple-element.138), channel_id=1, source_target_pairs={{0,6},{1,7},{2,4},{3,5},{4,2},{5,3},{6,0},{7,1},{8,14},{9,15},{10,... | collective-permute-start | bytes 1130504 | tf_op jit(solution)/shard_map/ppermute | solution.py:418
  67.6 27.6 %collective-permute-start.12 = (bf16[2,184,512]{2,1,0:T(8,128)(2,1)}, bf16[2,184,512]{2,1,0:T(8,128)(2,1)S(1)}, u32[]{:S(2)}, u32[]{:S(2)}) collective-permute-start(bf16[2,184,512]{2,1,0:T(8,128)(2,1)} %get-tuple-element.136), channel_id=1, source_target_pairs={{0,4},{1,5},{2,6},{3,7},{4,0},{5,1},{6,2},{7,3},{8,12},{9,13},{10,... | collective-permute-start | bytes 1130504 | tf_op jit(solution)/shard_map/ppermute | solution.py:418
  68.1 27.1 %collective-permute-start.11 = (bf16[2,184,512]{2,1,0:T(8,128)(2,1)}, bf16[2,184,512]{2,1,0:T(8,128)(2,1)S(1)}, u32[]{:S(2)}, u32[]{:S(2)}) collective-permute-start(bf16[2,184,512]{2,1,0:T(8,128)(2,1)} %get-tuple-element.134), channel_id=1, source_target_pairs={{0,2},{1,3},{2,0},{3,1},{4,6},{5,7},{6,4},{7,5},{8,10},{9,11},{10,... | collective-permute-start | bytes 1130504 | tf_op jit(solution)/shard_map/ppermute | solution.py:418
  83.8 23.6 %collective-permute-start.15 = (bf16[4,184,256]{2,1,0:T(8,128)(2,1)S(1)}, bf16[4,184,256]{2,1,0:T(8,128)(2,1)S(1)}, u32[]{:S(2)}, u32[]{:S(2)}) collective-permute-start(bf16[4,184,256]{2,1,0:T(8,128)(2,1)S(1)} %copy-done.38), channel_id=1, source_target_pairs={{0,8},{24,16},{1,9},{25,17},{2,10},{26,18},{3,11},{27,19},{4,12},{... | collective-permute-start | bytes 1130504 | tf_op jit(solution)/shard_map/ppermute | solution.py:380
  105.5 19.3 %collective-permute-start.18 = (bf16[2,184,512]{2,1,0:T(8,128)(2,1)}, bf16[2,184,512]{2,1,0:T(8,128)(2,1)S(1)}, u32[]{:S(2)}, u32[]{:S(2)}) collective-permute-start(bf16[2,184,512]{2,1,0:T(8,128)(2,1)} %get-tuple-element.152), channel_id=1, source_target_pairs={{0,4},{1,5},{2,6},{3,7},{4,0},{5,1},{6,2},{7,3},{8,12},{9,13},{10,... | collective-permute-start | bytes 1130504 | tf_op jit(solution)/shard_map/ppermute | solution.py:418
  106.0 18.9 %collective-permute-start.17 = (bf16[2,184,512]{2,1,0:T(8,128)(2,1)}, bf16[2,184,512]{2,1,0:T(8,128)(2,1)S(1)}, u32[]{:S(2)}, u32[]{:S(2)}) collective-permute-start(bf16[2,184,512]{2,1,0:T(8,128)(2,1)} %get-tuple-element.150), channel_id=1, source_target_pairs={{0,2},{1,3},{2,0},{3,1},{4,6},{5,7},{6,4},{7,5},{8,10},{9,11},{10,... | collective-permute-start | bytes 1130504 | tf_op jit(solution)/shard_map/ppermute | solution.py:418
  146.9 32.7 %collective-permute-start.34 = (bf16[4,184,512]{2,1,0:T(8,128)(2,1)}, bf16[4,184,512]{2,1,0:T(8,128)(2,1)S(1)}, u32[]{:S(2)}, u32[]{:S(2)}) collective-permute-start(bf16[4,184,512]{2,1,0:T(8,128)(2,1)} %get-tuple-element.197), channel_id=1, source_target_pairs={{0,1},{1,0},{2,3},{3,2},{4,5},{5,4},{6,7},{7,6},{8,9},{9,8},{10,11... | collective-permute-start | bytes 2261000 | tf_op jit(solution)/shard_map/ppermute | solution.py:363
  149.8 39.2 %collective-permute-start.33 = (bf16[4,184,512]{2,1,0:T(8,128)(2,1)}, bf16[4,184,512]{2,1,0:T(8,128)(2,1)S(1)}, u32[]{:S(2)}, u32[]{:S(2)}) collective-permute-start(bf16[4,184,512]{2,1,0:T(8,128)(2,1)} %get-tuple-element.197), channel_id=1, source_target_pairs={{8,1},{9,0},{10,3},{11,2},{12,5},{13,4},{14,7},{15,6},{16,25},{17,... | collective-permute-start | bytes 2261000 | tf_op jit(solution)/shard_map/ppermute | solution.py:380
  154.3 34.8 %collective-permute-start.32 = (bf16[4,184,512]{2,1,0:T(8,128)(2,1)S(1)}, bf16[4,184,512]{2,1,0:T(8,128)(2,1)S(1)}, u32[]{:S(2)}, u32[]{:S(2)}) collective-permute-start(bf16[4,184,512]{2,1,0:T(8,128)(2,1)S(1)} %copy-done), channel_id=1, source_target_pairs={{8,0},{16,24},{9,1},{17,25},{10,2},{18,26},{11,3},{19,27},{12,4},{... | collective-permute-start | bytes 2261000 | tf_op jit(solution)/shard_map/ppermute | solution.py:380
  161.9 17.0 %collective-permute-start.27 = (bf16[2,184,512]{2,1,0:T(8,128)(2,1)S(1)}, bf16[2,184,512]{2,1,0:T(8,128)(2,1)S(1)}, u32[]{:S(2)}, u32[]{:S(2)}) collective-permute-start(bf16[2,184,512]{2,1,0:T(8,128)(2,1)S(1)} %copy-done.39), channel_id=1, source_target_pairs={{0,4},{1,5},{2,6},{3,7},{4,0},{5,1},{6,2},{7,3},{8,12},{9,13},{10,... | collective-permute-start | bytes 1130504 | tf_op jit(solution)/shard_map/ppermute | solution.py:418
  162.0 17.3 %collective-permute-start.28 = (bf16[2,184,512]{2,1,0:T(8,128)(2,1)}, bf16[2,184,512]{2,1,0:T(8,128)(2,1)S(1)}, u32[]{:S(2)}, u32[]{:S(2)}) collective-permute-start(bf16[2,184,512]{2,1,0:T(8,128)(2,1)} %get-tuple-element.182), channel_id=1, source_target_pairs={{0,6},{1,7},{2,4},{3,5},{4,2},{5,3},{6,0},{7,1},{8,14},{9,15},{10,... | collective-permute-start | bytes 1130504 | tf_op jit(solution)/shard_map/ppermute | solution.py:418
  179.2 18.1 %collective-permute-start.30 = (bf16[2,184,512]{2,1,0:T(8,128)(2,1)}, bf16[2,184,512]{2,1,0:T(8,128)(2,1)}, u32[]{:S(2)}, u32[]{:S(2)}) collective-permute-start(bf16[2,184,512]{2,1,0:T(8,128)(2,1)} %get-tuple-element.191), channel_id=1, source_target_pairs={{0,4},{1,5},{2,6},{3,7},{4,0},{5,1},{6,2},{7,3},{8,12},{9,13},{10,... | collective-permute-start | bytes 1130504 | tf_op jit(solution)/shard_map/ppermute | solution.py:418
  180.0 18.7 %collective-permute-start.31 = (bf16[2,184,512]{2,1,0:T(8,128)(2,1)}, bf16[2,184,512]{2,1,0:T(8,128)(2,1)}, u32[]{:S(2)}, u32[]{:S(2)}) collective-permute-start(bf16[2,184,512]{2,1,0:T(8,128)(2,1)} %get-tuple-element.194), channel_id=1, source_target_pairs={{0,6},{1,7},{2,4},{3,5},{4,2},{5,3},{6,0},{7,1},{8,14},{9,15},{10,... | collective-permute-start | bytes 1130504 | tf_op jit(solution)/shard_map/ppermute | solution.py:418
  189.1 37.7 %collective-permute-start.42 = (bf16[4,184,512]{2,1,0:T(8,128)(2,1)}, bf16[4,184,512]{2,1,0:T(8,128)(2,1)S(1)}, u32[]{:S(2)}, u32[]{:S(2)}) collective-permute-start(bf16[4,184,512]{2,1,0:T(8,128)(2,1)} %get-tuple-element.201), channel_id=1, source_target_pairs={{0,1},{1,0},{2,3},{3,2},{4,5},{5,4},{6,7},{7,6},{8,9},{9,8},{10,11... | collective-permute-start | bytes 2261000 | tf_op jit(solution)/shard_map/ppermute | solution.py:363
  201.6 25.3 %collective-permute-start.43 = (bf16[4,184,512]{2,1,0:T(8,128)(2,1)}, bf16[4,184,512]{2,1,0:T(8,128)(2,1)S(1)}, u32[]{:S(2)}, u32[]{:S(2)}) collective-permute-start(bf16[4,184,512]{2,1,0:T(8,128)(2,1)} %get-tuple-element.202), channel_id=1, source_target_pairs={{0,1},{1,0},{2,3},{3,2},{4,5},{5,4},{6,7},{7,6},{8,9},{9,8},{10,11... | collective-permute-start | bytes 2261000 | tf_op jit(solution)/shard_map/ppermute | solution.py:363
  207.1 19.7 %collective-permute-start.40 = (bf16[4,184,256]{2,1,0:T(8,128)(2,1)S(1)}, bf16[4,184,256]{2,1,0:T(8,128)(2,1)S(1)}, u32[]{:S(2)}, u32[]{:S(2)}) collective-permute-start(bf16[4,184,256]{2,1,0:T(8,128)(2,1)S(1)} %copy-done.11), channel_id=1, source_target_pairs={{8,0},{16,24},{9,1},{17,25},{10,2},{18,26},{11,3},{19,27},{12,4},{... | collective-permute-start | bytes 1130504 | tf_op jit(solution)/shard_map/ppermute | solution.py:380
  (62 other events, 556.0 us)

commit v2 on v1

--- a/solution.py
+++ b/solution.py
@@ -13,10 +13,10 @@
 NLON = 1440
 MAIN = 256
 TAIL = 64
+SMALL = 60
 BF = jnp.bfloat16
 F32 = jnp.float32
 ANY = pl.BlockSpec(memory_space=pl.ANY)
-IN_SMEM = pl.BlockSpec(memory_space=pltpu.SMEM)
 IN_VMEM = pl.BlockSpec(memory_space=pltpu.VMEM)
 
 
@@ -43,6 +43,15 @@
     return forward, rows(1).astype(ml_dtypes.bfloat16)
 
 
+def number():
+    return lax.axis_index("lon")
+
+
+def in_polar_tile():
+    lat, lats = lax.axis_index("lat"), lax.axis_size("lat")
+    return (lat < lats // 4) | (lat >= lats - lats // 4)
+
+
 def copies(pairs, sems, base=0):
     made = [pltpu.make_async_copy(a, b, sems.at[base + i]) for i, (a, b) in enumerate(pairs)]
     for c in made:
@@ -55,8 +64,8 @@
         c.wait()
 
 
-def pack_kernel(cols, pad, count, sets, s, *refs):
-    me = s[0]
+def pack_kernel(cols, pad, count, sets, *refs):
+    me = number()
     n = len(sets)
     x, outs, (raw, work, in_sem, out_sem) = refs[0], refs[1 : 1 + 2 * n], refs[1 + 2 * n :]
     kinds = [(u, i, kind, q) for u, units in enumerate(sets) for i, (kind, q) in enumerate(units)]
@@ -89,7 +98,7 @@
     wait_all(stores)
 
 
-def select_kernel(groups, s, *refs):
+def select_kernel(groups, *refs):
     ins, ys, (held, in_sem, out_sem) = refs[: -groups - 3], refs[-groups - 3 : -3], refs[-3:]
 
     def move(own, par):
@@ -106,17 +115,17 @@
         move(*ins)
         return
 
-    @pl.when(s[1] == 1)
+    @pl.when(in_polar_tile())
     def _():
         move(*ins[:2])
 
-    @pl.when(s[1] != 1)
+    @pl.when(jnp.logical_not(in_polar_tile()))
     def _():
         move(*ins[2:])
 
 
-def filter_kernel(groups, s, cut, *refs):
-    me = s[0]
+def filter_kernel(groups, lane, cut, *refs):
+    me = number()
     ins, tables, zs = refs[:groups], refs[groups : groups + 4], refs[groups + 4 : 2 * groups + 4]
     work, done, held, in_sem, table_sem, out_sem = refs[2 * groups + 4 :][0:2] + (refs[2 * groups + 6 : -3],) + refs[-3:]
     count, pad, lanes = work.shape
@@ -130,7 +139,7 @@
     wait_all(loads)
     low = work[:half].astype(F32)
     high = work[half:].astype(F32)
-    cutoff = cut[...]
+    cutoff = cut[:, lane : lane + lanes]
 
     def side(values, parity):
         values = values.reshape(half * pad, lanes).astype(BF)
@@ -156,7 +165,7 @@
     wait_all(copies(pairs, out_sem))
 
 
-def gather_kernel(groups, s, *refs):
+def gather_kernel(groups, *refs):
     ins, outs, (held, in_sem, out_sem) = refs[:groups], refs[groups : groups + 2], refs[groups + 2 :]
     loads = copies([(ins[m], held.at[m]) for m in range(groups)], in_sem)
     stores = []
@@ -171,11 +180,11 @@
     return jnp.where(jnp.bitwise_and(rel, 1) == 0, own[spot], par[spot])
 
 
-def edge_kernel(cols, s, fo, fp, lo, lp, fto, ftp, lto, ltp, x_first, x_last, out_first, out_last):
-    me, polar = s[0], s[1]
+def edge_kernel(cols, fo, fp, lo, lp, fto, ftp, lto, ltp, x_first, x_last, out_first, out_last):
+    me, polar = number(), in_polar_tile()
     count = x_first.shape[1]
 
-    @pl.when(polar == 1)
+    @pl.when(polar)
     def _():
         for spot, own, par, tail_own, tail_par, at, out in (
             (0, fo, fp, fto, ftp, 0, out_first),
@@ -186,19 +195,22 @@
                 [row_of(own, par, rel), row_of(tail_own, tail_par, rel)[:, at : at + TAIL]], axis=-1
             )[1 : cols + 1]
 
-    @pl.when(polar != 1)
+    @pl.when(jnp.logical_not(polar))
     def _():
         out_first[...] = x_first[:, 0, :]
         out_last[...] = x_last[:, count - 1, :]
 
 
-def final_kernel(cols, count, tiles, places, s, north, south, sides, coef, *refs):
+def final_kernel(cols, count, tiles, span, places, north, south, sides, coef, *refs):
     tails = tiles // 4
-    parts, (x, out) = refs[:-11], refs[-11:-9]
+    x, out = refs[0], refs[-10]
+    parts = refs[1:]
     block, tail, own_rows, field, result, block_sem, tail_sem, row_sem, out_sem = refs[-9:]
-    me, polar = s[0], s[1]
+    me, polar = number(), in_polar_tile()
     width = 15
     groups = count // 2
+    begin, end = span
+    first, last = max(begin - 1, 0), min(end + 1, tiles)
 
     def sources(unit, place):
         number, i = places[unit]
@@ -223,28 +235,28 @@
         return pltpu.make_async_copy(x.at[:, pl.ds(q * count, count), :], own_rows.at[slot], row_sem.at[slot])
 
     def load(q):
-        @pl.when(polar == 1)
+        @pl.when(polar)
         def _():
             for c in main_copies(q):
                 c.start()
 
-        @pl.when(polar != 1)
+        @pl.when(jnp.logical_not(polar))
         def _():
             row_copy(q).start()
 
     def prepare(q):
         place = q % 3
 
-        @pl.when(polar == 1)
+        @pl.when(polar)
         def _():
             wait_all(main_copies(q))
-            if q % 4 == 0:
+            if q == max(first, q // 4 * 4):
                 wait_all(tail_copies(q // 4))
             at = q % 4 * TAIL
             rows = jnp.concatenate([block[q % 2], tail[q // 4, :, :, at : at + TAIL]], axis=-1)
             field[place] = jnp.swapaxes(rows, 0, 1)[: cols + 2]
 
-        @pl.when(polar != 1)
+        @pl.when(jnp.logical_not(polar))
         def _():
             row_copy(q).wait()
             field[place, 1 : cols + 1] = own_rows[q % 2]
@@ -254,22 +266,26 @@
     def store(q):
         return pltpu.make_async_copy(result.at[q % 2], out.at[:, pl.ds(q * count, count), :], out_sem.at[q % 2])
 
-    @pl.when(polar == 1)
+    @pl.when(polar)
     def _():
-        for t in range(tails):
+        for t in range(first // 4, (last - 1) // 4 + 1):
             for c in tail_copies(t):
                 c.start()
 
-    load(0)
-    load(1)
-    prepare(0)
+    load(first)
+    load(first + 1)
+    prepare(first)
+    if first < begin:
+        if first + 2 < last:
+            load(first + 2)
+        prepare(begin)
     spot = lax.broadcasted_iota(jnp.int32, (1, count, 1), 1)
-    for q in range(tiles):
-        if q + 2 < tiles:
+    for q in range(begin, end):
+        if q + 2 < last:
             load(q + 2)
-        if q + 1 < tiles:
+        if q + 1 < last:
             prepare(q + 1)
-        if q >= 2:
+        if q >= begin + 2:
             store(q - 2).wait()
         rows = slice(q * count, (q + 1) * count)
         k0, k1, k2, k3 = (coef[i, rows][None] for i in range(4))
@@ -293,7 +309,7 @@
 
         lax.fori_loop(0, cols // width, step, 0)
         store(q).start()
-    for q in range(max(tiles - 2, 0), tiles):
+    for q in range(max(end - 2, begin), end):
         store(q).wait()
 
 
@@ -318,10 +334,11 @@
     lat, me = lax.axis_index("lat"), lax.axis_index("lon")
     edge = lats // 4
     is_polar = (lat < edge) | (lat >= lats - edge)
-    flags = jnp.stack([me, is_polar.astype(jnp.int32)]).astype(jnp.int32)
     x = jnp.transpose(state, (1, 0, 2))
 
     helpers = [(i, i + edge) for i in range(edge)] + [(lats - 1 - i, lats - 1 - i - edge) for i in range(edge)]
+
+    back = [(b, a) for a, b in helpers]
 
     served = jnp.where(is_polar, lat, jnp.where(lat < lats // 2, lat - edge, lat + edge))
     served = jnp.where(served < lats // 2, served, served - lats // 2)
@@ -342,17 +359,18 @@
 
     ran = []
 
-    def call(kernel, arrays, specs, outs, name, scratch, after=(), out_specs=None):
+    def call(kernel, arrays, specs, outs, name, scratch, after=(), mib=60, aliases=None):
         results = pl.pallas_call(
             kernel,
-            in_specs=[IN_SMEM] + specs,
-            out_specs=out_specs or [ANY] * len(outs),
+            in_specs=specs,
+            out_specs=[ANY] * len(outs),
             out_shape=outs,
             scratch_shapes=scratch,
-            compiler_params=pltpu.CompilerParams(vmem_limit_bytes=60 * 2**20),
+            compiler_params=pltpu.CompilerParams(vmem_limit_bytes=mib * 2**20),
             cost_estimate=pl.CostEstimate(flops=1, bytes_accessed=1, transcendentals=0),
+            input_output_aliases=aliases or {},
             name=name,
-        )(tie(flags, *ran[-1:], *after), *arrays)
+        )(*arrays[:-1], tie(arrays[-1], *ran[-1:], *after))
         ran.append(results[0])
         return results
 
@@ -362,7 +380,7 @@
     def swapped(value):
         return lax.ppermute(value, "lon", [(i, i ^ 1) for i in range(count)])
 
-    def pack(sets):
+    def pack(sets, after=()):
         units = [unit for group in sets for unit in group]
         size = sum(count if kind == "main" else 4 * count for kind, _ in units)
         shapes = [block(groups, MAIN * len(group)) for group in sets for _ in range(2)]
@@ -372,6 +390,7 @@
                 pltpu.VMEM((cols, size, channels), BF), pltpu.VMEM((len(units), count, pad, MAIN), BF),
                 sems(len(units)), sems(len(units) * count),
             ],
+            after,
         )
         return [(outs[2 * u], outs[2 * u + 1]) for u in range(len(sets))]
 
@@ -384,29 +403,16 @@
         lanes = own[0].shape[-1]
         return call(
             functools.partial(select_kernel, groups), arrays, [ANY] * len(arrays), [block(2, lanes)] * groups, "select",
-            [pltpu.VMEM((groups, 2, pad, lanes), BF), sems(count), sems(groups)], after,
+            [pltpu.VMEM((groups, 2, pad, lanes), BF), sems(count), sems(groups)], after, SMALL,
         )
 
-    def cut_of(own_units, helped_units):
-        def lanes_of(units):
-            parts = []
-            for kind, q in units:
-                if kind == "main":
-                    parts.append(jnp.broadcast_to(cut_mine[q], (MAIN,)))
-                else:
-                    parts.append(jnp.repeat(cut_mine[4 * q : 4 * q + 4], TAIL))
-            return jnp.concatenate(parts)[None, :]
-
-        own = lanes_of(own_units)
-        return jnp.where(is_polar, own, lanes_of(helped_units)) if helped_units else own
-
-    def run_filter(pieces, cut):
-        lanes = cut.shape[-1]
+    def run_filter(pieces, number, after=()):
+        lanes = pieces[0].shape[-1]
         return call(
-            functools.partial(filter_kernel, groups), [cut, *pieces, *tables], [IN_VMEM] + [ANY] * (groups + 4),
+            functools.partial(filter_kernel, groups, cut_spot[number]), [cut_lanes, *pieces, *tables], [IN_VMEM] + [ANY] * (groups + 4),
             [block(2, lanes)] * groups, "filter",
             [pltpu.VMEM((count, pad, lanes), BF)] * 2 + [pltpu.VMEM(t.shape, BF) for t in tables]
-            + [sems(count), sems(4), sems(count)],
+            + [sems(count), sems(4), sems(count)], after, SMALL,
         )
 
     sent = []
@@ -419,31 +425,31 @@
             got.append(sent[-1])
         return got
 
-    def gather(pieces):
+    def gather(pieces, after=()):
         lanes = pieces[0].shape[-1]
         return call(
             functools.partial(gather_kernel, groups), pieces, [ANY] * groups, [block(groups, lanes)] * 2, "gather",
-            [pltpu.VMEM((groups, 2, pad, lanes), BF), sems(groups), sems(count)],
+            [pltpu.VMEM((groups, 2, pad, lanes), BF), sems(groups), sems(count)], after, SMALL,
         )
 
     mains = [("main", q) for q in range(tiles)]
     tail_units = [("tail", t) for t in range(tails)]
     order = [mains[tiles - 1], mains[0]] + mains[1 : tiles - 1]
     big = (tiles + tails) // 5
-    helped = [order[:big], order[big : big + 1]]
-    others = tail_units + order[big + 1 :]
-    shared = [others[:big], others[big : big + 1]]
-    lone = [others[i : i + big] for i in range(big + 1, len(others), big)]
-
-    sides = jnp.concatenate(
-        [
-            lax.ppermute(x[cols - 1 :], "lon", [(i, (i + 1) % count) for i in range(count)]),
-            lax.ppermute(x[:1], "lon", [((i + 1) % count, i) for i in range(count)]),
-        ],
-        axis=0,
+    helped, others = order[:big], tail_units + order[big:]
+    shared, lone, late = others[:big], others[big : 3 * big], others[3 * big :]
+
+    rows_own, rows_help, cut_spot = [], [], []
+    for units, served_units in [(shared, helped), (lone, lone), (late, late)]:
+        cut_spot.append(len(rows_own))
+        for listed, to in ((units, rows_own), (served_units, rows_help)):
+            for kind, q in listed:
+                to += [q] * MAIN if kind == "main" else [4 * q + i for i in range(4) for _ in range(TAIL)]
+    row_lanes = jnp.where(is_polar, np.array(rows_own, np.int32), np.array(rows_help, np.int32))
+    cut_lanes = jnp.sum(
+        jnp.where(jnp.arange(tiles)[:, None] == row_lanes[None, :], cut_mine[:, None], 0), axis=0, keepdims=True
     )
 
-    back = [(b, a) for a, b in helpers]
     done, places = [], {}
 
     def finish(units, pair):
@@ -451,37 +457,59 @@
             places[unit] = (len(done) // 2, i)
         done.extend(pair)
 
-    def give(units, zs, helped_units=()):
-        own, par = gather(zs)
+    def give(units, zs, after=()):
+        own, par = gather(zs, after)
         finish(units, (own, swapped(par)))
-        if helped_units:
-            finish(helped_units, hop(own, par, back))
 
     def apart(pair):
         return (pair[0], swapped(pair[1]))
 
-    first_helped, first_lone = pack([helped[0], lone[0]])
-    lifted = [hop(*first_helped, helpers)]
-    got_lone = [exchange(select(apart(first_lone)))]
-    later = pack(lone[1:] + shared + helped[1:])
-    more_lone, own = later[: len(lone) - 1], later[len(lone) - 1 : len(lone) + 1]
-    own = [apart(pair) for pair in own]
-    more_lone = [apart(pair) for pair in more_lone]
-    for pair in more_lone:
-        got_lone.append(exchange(select(pair)))
-    ys = select(own[0], lifted[0])
-    lifted.append(hop(*(tie(v, ys[0]) for v in later[-1]), helpers))
-    got = exchange(ys)
-    z_lone = [run_filter(g, cut_of(units, [])) for g, units in zip(got_lone, lone)]
-    zs = exchange(run_filter(got, cut_of(shared[0], helped[0])))
-    ys = select(own[1], lifted[1])
-    got = exchange(ys)
-    give(shared[0], zs, helped[0])
-    zs = exchange(run_filter(got, cut_of(shared[1], helped[1])))
-    z_lone = [exchange([tie(v, ran[-1]) for v in z]) for z in z_lone]
-    give(shared[1], zs, helped[1])
-    for z, units in zip(z_lone, lone):
-        give(units, z)
+    tile_rows = lat * rows + jnp.arange(rows, dtype=jnp.int32)
+    north_ratio, south_ratio = metric(tile_rows, nlat)
+    v = jnp.broadcast_to(viscosity[None, :], (rows, channels))
+    a, b = north_ratio[:, None] * v, south_ratio[:, None] * v
+    coef = jnp.stack([1.0 - 2.0 * v - a - b, v, a, b])
+
+    def flux(span, below, so_far=()):
+        return call(
+            functools.partial(final_kernel, cols, count, tiles, span, dict(places)),
+            [north, below, sides, coef, x, *done, *so_far],
+            [IN_VMEM] * 4 + [ANY] * (len(done) + len(so_far) + 1),
+            [jax.ShapeDtypeStruct((cols, rows, channels), F32)], "flux_step",
+            [
+                pltpu.VMEM((2, count, pad, MAIN), BF), pltpu.VMEM((tails, count, pad, MAIN), BF),
+                pltpu.VMEM((2, cols, count, channels), BF), pltpu.VMEM((3, cols + 2, count, channels), BF),
+                pltpu.VMEM((2, cols, count, channels), F32),
+                sems(2, count), sems(tails, count), sems(2), sems(2),
+            ],
+            aliases={5 + len(done): 0} if so_far else {},
+        )
+
+    up, mine = pack([helped, lone])
+    ys = select(apart(mine))
+    got_lone = exchange(ys)
+    lifted = hop(*(tie(v, ys[0]) for v in up), helpers)
+    own, mine = pack([shared, late])
+    own, mine = apart(own), apart(mine)
+    got = exchange(select(own, lifted, got_lone[1:]))
+    got_late = exchange(select(mine))
+    z = exchange(run_filter(got, 0))
+    z_lone = run_filter(got_lone, 1)
+    own, par = gather(z)
+    finish(shared, (own, swapped(par)))
+    finish(helped, hop(own, par, back))
+    z_lone = exchange(z_lone)
+    z_late = run_filter(got_late, 2)
+    give(lone, z_lone, done[2:4])
+    sides = jnp.concatenate(
+        [
+            lax.ppermute(tie(x[cols - 1 :], ran[-1]), "lon", [(i, (i + 1) % count) for i in range(count)]),
+            lax.ppermute(tie(x[:1], ran[-1]), "lon", [((i + 1) % count, i) for i in range(count)]),
+        ],
+        axis=0,
+    )
+
+    z_late = exchange(z_late)
 
     edge_arrays, edge_specs = [], []
     for unit in (mains[0], mains[tiles - 1], tail_units[0], tail_units[tails - 1]):
@@ -495,34 +523,23 @@
     first, last = pl.pallas_call(
         functools.partial(edge_kernel, cols),
         grid=(1,),
-        in_specs=[IN_SMEM] + edge_specs + [tile_spec(0), tile_spec(tiles - 1)],
+        in_specs=edge_specs + [tile_spec(0), tile_spec(tiles - 1)],
         out_specs=[pl.BlockSpec((cols, channels), lambda i: (0, 0))] * 2,
         out_shape=[jax.ShapeDtypeStruct((cols, channels), BF)] * 2,
         compiler_params=pltpu.CompilerParams(vmem_limit_bytes=60 * 2**20),
         cost_estimate=pl.CostEstimate(flops=1, bytes_accessed=1, transcendentals=0),
         name="edges",
-    )(flags, *edge_arrays, x, x)
+    )(*edge_arrays, x, x)
     north = lax.ppermute(last, "lat", [(i, i + 1) for i in range(lats - 1)]).reshape(cols, 1, channels)
     south = lax.ppermute(first, "lat", [(i + 1, i) for i in range(lats - 1)]).reshape(cols, 1, channels)
 
-    tile_rows = lat * rows + jnp.arange(rows, dtype=jnp.int32)
-    north_ratio, south_ratio = metric(tile_rows, nlat)
-    v = jnp.broadcast_to(viscosity[None, :], (rows, channels))
-    a, b = north_ratio[:, None] * v, south_ratio[:, None] * v
-    coef = jnp.stack([1.0 - 2.0 * v - a - b, v, a, b])
-
-    updated = call(
-        functools.partial(final_kernel, cols, count, tiles, places),
-        [north, south, sides, coef, *done, x],
-        [IN_VMEM] * 4 + [ANY] * (len(done) + 1),
-        [jax.ShapeDtypeStruct((cols, rows, channels), F32)], "flux_step",
-        [
-            pltpu.VMEM((2, count, pad, MAIN), BF), pltpu.VMEM((tails, count, pad, MAIN), BF),
-            pltpu.VMEM((2, cols, count, channels), BF), pltpu.VMEM((3, cols + 2, count, channels), BF),
-            pltpu.VMEM((2, cols, count, channels), F32),
-            sems(2, count), sems(tails, count), sems(2), sems(2),
-        ],
-    )[0]
+    ready = 0
+    while all(mains[q] in places for q in range(ready + 2)):
+        ready += 1
+    partly = flux((0, ready), north)
+    give(late, z_late, [south])
+    (updated,) = flux((ready, tiles), south, partly)
+
     return jnp.transpose(updated, (1, 0, 2))
 
 

time: 249 us -> 218 us (0.88)
  waiting for transfers between devices: 86.2 us -> 76 us
  starting transfers between devices: 52 us -> 43 us
  Pallas kernels: 88.1 us -> 81.1 us
  local copies, waits for them, and re-layouts: 15.6 us -> 13 us
    ppermute x24 -> x18, waiting for transfers between devices: 58.7 us -> 38.9 us  [exchange(): lax.ppermute(value, 'lon', [(i, i ^ 2 * m) for i in range(count)])]
    ppermute x24 -> x18, starting transfers between devices: 30.7 us -> 23.1 us  [exchange(): lax.ppermute(value, 'lon', [(i, i ^ 2 * m) for i in range(count)])]
    pallas_call x15 -> x13, Pallas kernels: 84.7 us -> 77.7 us  [call(): pl.pallas_call(kernel, in_specs=specs, out_specs=[ANY] * len(outs), out_s...]
    ppermute x4 -> x2, waiting for transfers between devices: 6.67 us -> 13.1 us  [hop(): lax.ppermute(par, ('lat', 'lon'), crossed)]
    unnamed x84 -> x67, local copies, waits for them, and re-layouts: 6.83 us -> 10.1 us
    ppermute x8 -> x6, waiting for transfers between devices: 2.09 us -> 5.22 us  [swapped(): return lax.ppermute(value, 'lon', [(i, i ^ 1) for i in range(count)])]
    ppermute x4 -> x2, starting transfers between devices: 5.97 us -> 3 us  [hop(): lax.ppermute(own, 'lat', pairs)]
    ppermute x1, starting transfers between devices: 2.98 us -> 5.49 us  [per_device(): lax.ppermute(last, 'lat', [(i, i + 1) for i in range(lats - 1)])]
  transfers between devices with their start and end apart: 44 -> 32, of which waited for: 18 -> 17; matrix products, arithmetic and copies ran while one was open for 4% -> 2% of each run, Pallas kernels for 19% -> 25%
where the time goes in v2:
time: 218 us; the launch traced here: 216 us
  Pallas kernels  81.1 us (37%)
  waiting for transfers between devices  76 us (35%)
  starting transfers between devices  43 us (20%)
  local copies, waits for them, and re-layouts  13 us (6%)
    pallas_call x13, Pallas kernels, call(): pl.pallas_call(kernel, in_specs=specs, out_specs=[ANY] * len(outs), out_s...  77.7 us
    ppermute x18, waiting for transfers between devices, exchange(): lax.ppermute(value, 'lon', [(i, i ^ 2 * m) for i in range(count)])  38.9 us
    ppermute x18, starting transfers between devices, exchange(): lax.ppermute(value, 'lon', [(i, i ^ 2 * m) for i in range(count)])  23.1 us
    ppermute x2, waiting for transfers between devices, hop(): lax.ppermute(own, 'lat', pairs)  15.6 us
    ppermute x2, waiting for transfers between devices, hop(): lax.ppermute(par, ('lat', 'lon'), crossed)  13.1 us
    unnamed x67, local copies, waits for them, and re-layouts  10.1 us
    ppermute x2, starting transfers between devices, hop(): lax.ppermute(par, ('lat', 'lon'), crossed)  5.93 us
    ppermute x1, starting transfers between devices, per_device(): lax.ppermute(last, 'lat', [(i, i + 1) for i in range(lats - 1)])  5.49 us
  transfers between devices with their start and end apart: 32, of which 17 were waited for; matrix products, arithmetic and copies ran while one was open for 2% of the time, Pallas kernels for 25%

profile of v2, /device:TPU:0, one launch (start us, length us, event | category | flops | bytes accessed | tf_op | source)
XLA Modules:
  0.0 215.6 jit_solution(2781296337627769693)
XLA Ops:
  0.0 5.6 %pack.2 = (bf16[4,184,512]{2,1,0:T(8,128)(2,1)}, bf16[4,184,512]{2,1,0:T(8,128)(2,1)}, bf16[4,184,1024]{2,1,0:T(8,128)(2,1)}, bf16[4,184,1024]{2,1,0:T(8,128)(2,1)}) custom-call(bf16[180,64,320]{2,1,0:T(8,128)(2,1)} %bitcast.5), custom_call_target="tpu_custom_call" | custom-call | flops 1 | bytes 1 | tf_op jit(solution)/shard_map/pack/pallas_call | solution.py:363
  6.1 3.2 %collective-permute-done.refs_1_ = bf16[4,184,1024]{2,1,0:T(8,128)(2,1)S(1)} collective-permute-done((bf16[4,184,1024]{2,1,0:T(8,128)(2,1)}, bf16[4,184,1024]{2,1,0:T(8,128)(2,1)S(1)}, u32[]{:S(2)}, u32[]{:S(2)}) %collective-permute-start) | collective-permute-done | bytes 1507360 | tf_op jit(solution)/shard_map/ppermute | solution.py:381
  10.4 3.0 %select.3 = (bf16[2,184,1024]{2,1,0:T(8,128)(2,1)}, bf16[2,184,1024]{2,1,0:T(8,128)(2,1)}, bf16[2,184,1024]{2,1,0:T(8,128)(2,1)}, bf16[2,184,1024]{2,1,0:T(8,128)(2,1)}) custom-call(bf16[4,184,1024]{2,1,0:T(8,128)(2,1)} %get-tuple-element.76.refs_0_, bf16[4,184,1024]{2,1,0:T(8,128)(2,1)} %copy-done.4), custom_call_target="tpu_custom_call" | custom-call | flops 1 | bytes 1 | tf_op jit(solution)/shard_map/select/pallas_call | solution.py:363
  13.4 4.6 %collective-permute-start.3 = (bf16[4,184,512]{2,1,0:T(8,128)(2,1)S(1)}, bf16[4,184,512]{2,1,0:T(8,128)(2,1)S(1)}, u32[]{:S(2)}, u32[]{:S(2)}) collective-permute-start(bf16[4,184,512]{2,1,0:T(8,128)(2,1)S(1)} %copy-done.31), channel_id=1, source_target_pairs={{0,9},{1,8},{2,11},{3,10},{4,13},{5,12},{6,15},{7,14},{24,17},{25,... | collective-permute-start | bytes 2261000 | tf_op jit(solution)/shard_map/ppermute | solution.py:399
  23.2 5.8 %pack.3 = (bf16[4,184,512]{2,1,0:T(8,128)(2,1)}, bf16[4,184,512]{2,1,0:T(8,128)(2,1)}, bf16[4,184,512]{2,1,0:T(8,128)(2,1)}, bf16[4,184,512]{2,1,0:T(8,128)(2,1)}) custom-call(bf16[180,64,320]{2,1,0:T(8,128)(2,1)} %bitcast.6), custom_call_target="tpu_custom_call" | custom-call | flops 1 | bytes 1 | tf_op jit(solution)/shard_map/pack/pallas_call | solution.py:363
  29.0 6.2 %collective-permute-done.3.refs_3_ = bf16[4,184,512]{2,1,0:T(8,128)(2,1)S(1)} collective-permute-done((bf16[4,184,512]{2,1,0:T(8,128)(2,1)S(1)}, bf16[4,184,512]{2,1,0:T(8,128)(2,1)S(1)}, u32[]{:S(2)}, u32[]{:S(2)}) %collective-permute-start.3) | collective-permute-done | bytes 753696 | tf_op jit(solution)/shard_map/ppermute | solution.py:399
  35.2 2.8 %collective-permute-done.4.refs_1_ = bf16[2,184,1024]{2,1,0:T(8,128)(2,1)S(1)} collective-permute-done((bf16[2,184,1024]{2,1,0:T(8,128)(2,1)}, bf16[2,184,1024]{2,1,0:T(8,128)(2,1)S(1)}, u32[]{:S(2)}, u32[]{:S(2)}) %collective-permute-start.4) | collective-permute-done | bytes 753696 | tf_op jit(solution)/shard_map/ppermute | solution.py:424
  38.9 17.4 %collective-permute-done.5.refs_2_ = bf16[2,184,1024]{2,1,0:T(8,128)(2,1)} collective-permute-done((bf16[2,184,1024]{2,1,0:T(8,128)(2,1)}, bf16[2,184,1024]{2,1,0:T(8,128)(2,1)}, u32[]{:S(2)}, u32[]{:S(2)}) %collective-permute-start.5) | collective-permute-done | bytes 753696 | tf_op jit(solution)/shard_map/ppermute | solution.py:424
  58.1 2.4 %select.4 = (bf16[2,184,512]{2,1,0:T(8,128)(2,1)}, bf16[2,184,512]{2,1,0:T(8,128)(2,1)}, bf16[2,184,512]{2,1,0:T(8,128)(2,1)}, bf16[2,184,512]{2,1,0:T(8,128)(2,1)}) custom-call(bf16[4,184,512]{2,1,0:T(8,128)(2,1)} %get-tuple-element.82.refs_0_, bf16[4,184,512]{2,1,0:T(8,128)(2,1)} %copy-done.11, bf16[4,184,512]{2,1,0:T(8,128)(2,1)} %copy-done.8, ...), custom_call_target="tpu_custom_call" | custom-call | flops 1 | bytes 1 | tf_op jit(solution)/shard_map/select/pallas_call | solution.py:363
  65.1 2.3 %select.5 = (bf16[2,184,512]{2,1,0:T(8,128)(2,1)}, bf16[2,184,512]{2,1,0:T(8,128)(2,1)}, bf16[2,184,512]{2,1,0:T(8,128)(2,1)}, bf16[2,184,512]{2,1,0:T(8,128)(2,1)}) custom-call(bf16[4,184,512]{2,1,0:T(8,128)(2,1)} %get-tuple-element.98.refs_0_, bf16[4,184,512]{2,1,0:T(8,128)(2,1)} %copy-done.6), custom_call_target="tpu_custom_call" | custom-call | flops 1 | bytes 1 | tf_op jit(solution)/shard_map/select/pallas_call | solution.py:363
  67.5 5.0 %collective-permute-done.7.refs_1_ = bf16[2,184,512]{2,1,0:T(8,128)(2,1)S(1)} collective-permute-done((bf16[2,184,512]{2,1,0:T(8,128)(2,1)}, bf16[2,184,512]{2,1,0:T(8,128)(2,1)S(1)}, u32[]{:S(2)}, u32[]{:S(2)}) %collective-permute-start.7) | collective-permute-done | bytes 376864 | tf_op jit(solution)/shard_map/ppermute | solution.py:424
  72.5 5.5 %collective-permute-done.8.refs_2_ = bf16[2,184,512]{2,1,0:T(8,128)(2,1)S(1)} collective-permute-done((bf16[2,184,512]{2,1,0:T(8,128)(2,1)}, bf16[2,184,512]{2,1,0:T(8,128)(2,1)S(1)}, u32[]{:S(2)}, u32[]{:S(2)}) %collective-permute-start.8) | collective-permute-done | bytes 376864 | tf_op jit(solution)/shard_map/ppermute | solution.py:424
  83.8 8.0 %filter.3 = (bf16[2,184,512]{2,1,0:T(8,128)(2,1)}, bf16[2,184,512]{2,1,0:T(8,128)(2,1)}, bf16[2,184,512]{2,1,0:T(8,128)(2,1)}, bf16[2,184,512]{2,1,0:T(8,128)(2,1)}) custom-call(s32[1,2048]{1,0:T(1,128)} %bitcast.14, bf16[2,184,512]{2,1,0:T(8,128)(2,1)} %get-tuple-element.91.refs_0_, bf16[2,184,512]{2,1,0:T(8,128)(2,1)} %copy-done.14, ...), custom_call_target="tpu_custom_call" | custom-call | flops 1 | bytes 1 | tf_op jit(solution)/shard_map/filter/pallas_call | solution.py:363
  94.2 4.5 %collective-permute-done.13.refs_2_ = bf16[2,184,512]{2,1,0:T(8,128)(2,1)S(1)} collective-permute-done((bf16[2,184,512]{2,1,0:T(8,128)(2,1)}, bf16[2,184,512]{2,1,0:T(8,128)(2,1)S(1)}, u32[]{:S(2)}, u32[]{:S(2)}) %collective-permute-start.13) | collective-permute-done | bytes 376864 | tf_op jit(solution)/shard_map/ppermute | solution.py:424
  98.7 2.5 %collective-permute-start.14 = (bf16[2,184,512]{2,1,0:T(8,128)(2,1)}, bf16[2,184,512]{2,1,0:T(8,128)(2,1)S(1)}, u32[]{:S(2)}, u32[]{:S(2)}) collective-permute-start(bf16[2,184,512]{2,1,0:T(8,128)(2,1)} %get-tuple-element.111), channel_id=1, source_target_pairs={{0,4},{1,5},{2,6},{3,7},{4,0},{5,1},{6,2},{7,3},{8,12},{9,13},{10,... | collective-permute-start | bytes 1130504 | tf_op jit(solution)/shard_map/ppermute | solution.py:424
  102.4 11.7 %filter.4 = (bf16[2,184,1024]{2,1,0:T(8,128)(2,1)}, bf16[2,184,1024]{2,1,0:T(8,128)(2,1)}, bf16[2,184,1024]{2,1,0:T(8,128)(2,1)}, bf16[2,184,1024]{2,1,0:T(8,128)(2,1)}) custom-call(s32[1,2048]{1,0:T(1,128)} %bitcast.15, bf16[2,184,1024]{2,1,0:T(8,128)(2,1)} %get-tuple-element.80.refs_0_, bf16[2,184,1024]{2,1,0:T(8,128)(2,1)} %copy-done.12, ...), custom_call_target="tpu_custom_call" | custom-call | flops 1 | bytes 1 | tf_op jit(solution)/shard_map/filter/pallas_call | solution.py:363
  124.3 7.9 %filter.5 = (bf16[2,184,512]{2,1,0:T(8,128)(2,1)}, bf16[2,184,512]{2,1,0:T(8,128)(2,1)}, bf16[2,184,512]{2,1,0:T(8,128)(2,1)}, bf16[2,184,512]{2,1,0:T(8,128)(2,1)}) custom-call(s32[1,2048]{1,0:T(1,128)} %bitcast.16, bf16[2,184,512]{2,1,0:T(8,128)(2,1)} %get-tuple-element.101.refs_0_, bf16[2,184,512]{2,1,0:T(8,128)(2,1)} %copy-done.19, ...), custom_call_target="tpu_custom_call" | custom-call | flops 1 | bytes 1 | tf_op jit(solution)/shard_map/filter/pallas_call | solution.py:363
  132.2 6.9 %collective-permute-done.18.fp.lp.refs_4_ = bf16[4,184,512]{2,1,0:T(8,128)(2,1)S(1)} collective-permute-done((bf16[4,184,512]{2,1,0:T(8,128)(2,1)}, bf16[4,184,512]{2,1,0:T(8,128)(2,1)S(1)}, u32[]{:S(2)}, u32[]{:S(2)}) %collective-permute-start.18) | collective-permute-done | bytes 753696 | tf_op jit(solution)/shard_map/ppermute | solution.py:399
  139.1 15.6 %collective-permute-done.17.fo.lo.refs_3_ = bf16[4,184,512]{2,1,0:T(8,128)(2,1)S(1)} collective-permute-done((bf16[4,184,512]{2,1,0:T(8,128)(2,1)}, bf16[4,184,512]{2,1,0:T(8,128)(2,1)S(1)}, u32[]{:S(2)}, u32[]{:S(2)}) %collective-permute-start.17) | collective-permute-done | bytes 753696 | tf_op jit(solution)/shard_map/ppermute | solution.py:399
  156.5 2.8 %gather.4 = (bf16[4,184,1024]{2,1,0:T(8,128)(2,1)}, bf16[4,184,1024]{2,1,0:T(8,128)(2,1)}) custom-call(bf16[2,184,1024]{2,1,0:T(8,128)(2,1)} %get-tuple-element.117.refs_0_, bf16[2,184,1024]{2,1,0:T(8,128)(2,1)} %copy-done.10, bf16[2,184,1024]{2,1,0:T(8,128)(2,1)} %collective-permute-done.23.refs_2_, bf16[2,184,1024]{2,1,0:T(8,128)(2,1)} %copy-done.9), custom_call_target="tpu_custom_call" | custom-call | flops 1 | bytes 1 | tf_op jit(solution)/shard_map/gather/pallas_call | solution.py:363
  166.6 3.4 %edges.1 = (bf16[180,320]{1,0:T(8,128)(2,1)}, bf16[180,320]{1,0:T(8,128)(2,1)}) custom-call(bf16[4,184,512]{2,1,0:T(8,128)(2,1)} %copy-done.1, bf16[4,184,512]{2,1,0:T(8,128)(2,1)} %copy-done, bf16[4,184,512]{2,1,0:T(8,128)(2,1)} %copy-done.1, bf16[4,184,512]{2,1,0:T(8,128)(2,1)} %copy-done, bf16[4,184,512]{2,1,0:T(8,128)(2,1)} %get-tuple-element.119.fto.lto.refs_1_, ...), custom_call_target="tpu_custom_call" | custom-call | flops 1 | bytes 1 | tf_op jit(solution)/shard_map/edges/pallas_call | solution.py:523
  171.0 5.5 %collective-permute-start.20 = (bf16[180,320]{1,0:T(8,128)(2,1)}, bf16[180,320]{1,0:T(8,128)(2,1)S(1)}, u32[]{:S(2)}, u32[]{:S(2)}) collective-permute-start(bf16[180,320]{1,0:T(8,128)(2,1)} %get-tuple-element.121), channel_id=1, source_target_pairs={{0,8},{8,16},{16,24},{1,9},{9,17},{17,25},{2,10},{10,18},{18,26},{... | collective-permute-start | bytes 345608 | tf_op jit(solution)/shard_map/ppermute | solution.py:533
  182.8 11.7 %flux_step.2.refs_9_ = f32[180,64,320]{2,1,0:T(8,128)} custom-call(bf16[180,1,320]{2,1,0:T(2,128)(2,1)} %copy.17.north.south, bf16[180,1,320]{2,1,0:T(2,128)(2,1)} %copy.17.north.south, bf16[2,64,320]{2,1,0:T(8,128)(2,1)} %copy-done.13, f32[4,64,320]{2,1,0:T(8,128)} %pad_maximum_fusion.coef, bf16[180,64,320]{2,1,0:T(8,128)(2,1)} %bitcast.10, ...), custom_call_target="tpu_custom_call" | custom-call | flops 1 | bytes 1 | tf_op jit(solution)/shard_map/flux_step/pallas_call | solution.py:363
  203.2 12.2 %flux_step.3 = f32[180,64,320]{2,1,0:T(8,128)} custom-call(bf16[180,1,320]{2,1,0:T(2,128)(2,1)} %copy.17.north.south, bf16[180,1,320]{2,1,0:T(2,128)(2,1)} %copy.18.south, bf16[2,64,320]{2,1,0:T(8,128)(2,1)} %copy-done.13, f32[4,64,320]{2,1,0:T(8,128)} %pad_maximum_fusion.coef, bf16[180,64,320]{2,1,0:T(8,128)(2,1)} %bitcast.11, ...), custom_call_target="tpu_custom_call", output_to_operand_aliasing={{}: (13, {})} | custom-call | flops 1 | bytes 1 | tf_op jit(solution)/shard_map/flux_step/pallas_call | solution.py:363
  (136 shorter events, 58.5 us)
Async XLA Ops:
  13.4 21.8 %collective-permute-start.3 = (bf16[4,184,512]{2,1,0:T(8,128)(2,1)S(1)}, bf16[4,184,512]{2,1,0:T(8,128)(2,1)S(1)}, u32[]{:S(2)}, u32[]{:S(2)}) collective-permute-start(bf16[4,184,512]{2,1,0:T(8,128)(2,1)S(1)} %copy-done.31), channel_id=1, source_target_pairs={{0,9},{1,8},{2,11},{3,10},{4,13},{5,12},{6,15},{7,14},{24,17},{25,... | collective-permute-start | bytes 2261000 | tf_op jit(solution)/shard_map/ppermute | solution.py:399
  18.1 19.9 %collective-permute-start.4 = (bf16[2,184,1024]{2,1,0:T(8,128)(2,1)}, bf16[2,184,1024]{2,1,0:T(8,128)(2,1)S(1)}, u32[]{:S(2)}, u32[]{:S(2)}) collective-permute-start(bf16[2,184,1024]{2,1,0:T(8,128)(2,1)} %get-tuple-element.87), channel_id=1, source_target_pairs={{0,2},{1,3},{2,0},{3,1},{4,6},{5,7},{6,4},{7,5},{8,10},{9,11},{10,... | collective-permute-start | bytes 2261000 | tf_op jit(solution)/shard_map/ppermute | solution.py:424
  19.6 36.7 %collective-permute-start.2 = (bf16[4,184,512]{2,1,0:T(8,128)(2,1)S(1)}, bf16[4,184,512]{2,1,0:T(8,128)(2,1)S(1)}, u32[]{:S(2)}, u32[]{:S(2)}) collective-permute-start(bf16[4,184,512]{2,1,0:T(8,128)(2,1)S(1)} %copy-done.30), channel_id=1, source_target_pairs={{0,8},{24,16},{1,9},{25,17},{2,10},{26,18},{3,11},{27,19},{4,12},{... | collective-permute-start | bytes 2261000 | tf_op jit(solution)/shard_map/ppermute | solution.py:399
  21.2 35.2 %collective-permute-start.5 = (bf16[2,184,1024]{2,1,0:T(8,128)(2,1)}, bf16[2,184,1024]{2,1,0:T(8,128)(2,1)}, u32[]{:S(2)}, u32[]{:S(2)}) collective-permute-start(bf16[2,184,1024]{2,1,0:T(8,128)(2,1)} %get-tuple-element.88), channel_id=1, source_target_pairs={{0,4},{1,5},{2,6},{3,7},{4,0},{5,1},{6,2},{7,3},{8,12},{9,13},{10,... | collective-permute-start | bytes 2261000 | tf_op jit(solution)/shard_map/ppermute | solution.py:424
  22.7 33.6 %collective-permute-start.6 = (bf16[2,184,1024]{2,1,0:T(8,128)(2,1)}, bf16[2,184,1024]{2,1,0:T(8,128)(2,1)}, u32[]{:S(2)}, u32[]{:S(2)}) collective-permute-start(bf16[2,184,1024]{2,1,0:T(8,128)(2,1)} %get-tuple-element.89), channel_id=1, source_target_pairs={{0,6},{1,7},{2,4},{3,5},{4,2},{5,3},{6,0},{7,1},{8,14},{9,15},{10,... | collective-permute-start | bytes 2261000 | tf_op jit(solution)/shard_map/ppermute | solution.py:424
  35.2 21.1 %collective-permute-start.1 = (bf16[4,184,512]{2,1,0:T(8,128)(2,1)}, bf16[4,184,512]{2,1,0:T(8,128)(2,1)S(1)}, u32[]{:S(2)}, u32[]{:S(2)}) collective-permute-start(bf16[4,184,512]{2,1,0:T(8,128)(2,1)} %get-tuple-element.83), channel_id=1, source_target_pairs={{0,1},{1,0},{2,3},{3,2},{4,5},{5,4},{6,7},{7,6},{8,9},{9,8},{10,11... | collective-permute-start | bytes 2261000 | tf_op jit(solution)/shard_map/ppermute | solution.py:381
  38.9 25.4 %collective-permute-start.10 = (bf16[4,184,512]{2,1,0:T(8,128)(2,1)}, bf16[4,184,512]{2,1,0:T(8,128)(2,1)S(1)}, u32[]{:S(2)}, u32[]{:S(2)}) collective-permute-start(bf16[4,184,512]{2,1,0:T(8,128)(2,1)} %get-tuple-element.99), channel_id=1, source_target_pairs={{0,1},{1,0},{2,3},{3,2},{4,5},{5,4},{6,7},{7,6},{8,9},{9,8},{10,11... | collective-permute-start | bytes 2261000 | tf_op jit(solution)/shard_map/ppermute | solution.py:381
  61.1 16.9 %collective-permute-start.8 = (bf16[2,184,512]{2,1,0:T(8,128)(2,1)}, bf16[2,184,512]{2,1,0:T(8,128)(2,1)S(1)}, u32[]{:S(2)}, u32[]{:S(2)}) collective-permute-start(bf16[2,184,512]{2,1,0:T(8,128)(2,1)} %get-tuple-element.95), channel_id=1, source_target_pairs={{0,4},{1,5},{2,6},{3,7},{4,0},{5,1},{6,2},{7,3},{8,12},{9,13},{10,... | collective-permute-start | bytes 1130504 | tf_op jit(solution)/shard_map/ppermute | solution.py:424
  62.6 16.9 %collective-permute-start.9 = (bf16[2,184,512]{2,1,0:T(8,128)(2,1)}, bf16[2,184,512]{2,1,0:T(8,128)(2,1)S(1)}, u32[]{:S(2)}, u32[]{:S(2)}) collective-permute-start(bf16[2,184,512]{2,1,0:T(8,128)(2,1)} %get-tuple-element.97), channel_id=1, source_target_pairs={{0,6},{1,7},{2,4},{3,5},{4,2},{5,3},{6,0},{7,1},{8,14},{9,15},{10,... | collective-permute-start | bytes 1130504 | tf_op jit(solution)/shard_map/ppermute | solution.py:424
  81.3 17.4 %collective-permute-start.13 = (bf16[2,184,512]{2,1,0:T(8,128)(2,1)}, bf16[2,184,512]{2,1,0:T(8,128)(2,1)S(1)}, u32[]{:S(2)}, u32[]{:S(2)}) collective-permute-start(bf16[2,184,512]{2,1,0:T(8,128)(2,1)} %get-tuple-element.110), channel_id=1, source_target_pairs={{0,4},{1,5},{2,6},{3,7},{4,0},{5,1},{6,2},{7,3},{8,12},{9,13},{10,... | collective-permute-start | bytes 1130504 | tf_op jit(solution)/shard_map/ppermute | solution.py:424
  81.8 19.4 %collective-permute-start.11 = (bf16[2,184,512]{2,1,0:T(8,128)(2,1)}, bf16[2,184,512]{2,1,0:T(8,128)(2,1)S(1)}, u32[]{:S(2)}, u32[]{:S(2)}) collective-permute-start(bf16[2,184,512]{2,1,0:T(8,128)(2,1)} %get-tuple-element.106), channel_id=1, source_target_pairs={{0,2},{1,3},{2,0},{3,1},{4,6},{5,7},{6,4},{7,5},{8,10},{9,11},{10,... | collective-permute-start | bytes 1130504 | tf_op jit(solution)/shard_map/ppermute | solution.py:424
  92.3 21.8 %collective-permute-start.16 = (bf16[2,184,512]{2,1,0:T(8,128)(2,1)}, bf16[2,184,512]{2,1,0:T(8,128)(2,1)S(1)}, u32[]{:S(2)}, u32[]{:S(2)}) collective-permute-start(bf16[2,184,512]{2,1,0:T(8,128)(2,1)} %get-tuple-element.115), channel_id=1, source_target_pairs={{0,6},{1,7},{2,4},{3,5},{4,2},{5,3},{6,0},{7,1},{8,14},{9,15},{10,... | collective-permute-start | bytes 1130504 | tf_op jit(solution)/shard_map/ppermute | solution.py:424
  98.7 15.4 %collective-permute-start.14 = (bf16[2,184,512]{2,1,0:T(8,128)(2,1)}, bf16[2,184,512]{2,1,0:T(8,128)(2,1)S(1)}, u32[]{:S(2)}, u32[]{:S(2)}) collective-permute-start(bf16[2,184,512]{2,1,0:T(8,128)(2,1)} %get-tuple-element.111), channel_id=1, source_target_pairs={{0,4},{1,5},{2,6},{3,7},{4,0},{5,1},{6,2},{7,3},{8,12},{9,13},{10,... | collective-permute-start | bytes 1130504 | tf_op jit(solution)/shard_map/ppermute | solution.py:424
  101.2 12.9 %collective-permute-start.12 = (bf16[2,184,512]{2,1,0:T(8,128)(2,1)}, bf16[2,184,512]{2,1,0:T(8,128)(2,1)S(1)}, u32[]{:S(2)}, u32[]{:S(2)}) collective-permute-start(bf16[2,184,512]{2,1,0:T(8,128)(2,1)} %get-tuple-element.107), channel_id=1, source_target_pairs={{0,2},{1,3},{2,0},{3,1},{4,6},{5,7},{6,4},{7,5},{8,10},{9,11},{10,... | collective-permute-start | bytes 1130504 | tf_op jit(solution)/shard_map/ppermute | solution.py:424
  118.0 21.1 %collective-permute-start.18 = (bf16[4,184,512]{2,1,0:T(8,128)(2,1)}, bf16[4,184,512]{2,1,0:T(8,128)(2,1)S(1)}, u32[]{:S(2)}, u32[]{:S(2)}) collective-permute-start(bf16[4,184,512]{2,1,0:T(8,128)(2,1)} %get-tuple-element.120), channel_id=1, source_target_pairs={{8,1},{9,0},{10,3},{11,2},{12,5},{13,4},{14,7},{15,6},{16,25},{17,... | collective-permute-start | bytes 2261000 | tf_op jit(solution)/shard_map/ppermute | solution.py:399
  119.3 35.5 %collective-permute-start.17 = (bf16[4,184,512]{2,1,0:T(8,128)(2,1)}, bf16[4,184,512]{2,1,0:T(8,128)(2,1)S(1)}, u32[]{:S(2)}, u32[]{:S(2)}) collective-permute-start(bf16[4,184,512]{2,1,0:T(8,128)(2,1)} %get-tuple-element.119.fto.lto.refs_1_), channel_id=1, source_target_pairs={{8,0},{16,24},{9,1},{17,25},{10,2},{18,26},{11,3},{19,27},{12,4},{... | collective-permute-start | bytes 2261000 | tf_op jit(solution)/shard_map/ppermute | solution.py:399
  120.8 34.0 %collective-permute-start.24 = (bf16[2,184,1024]{2,1,0:T(8,128)(2,1)}, bf16[2,184,1024]{2,1,0:T(8,128)(2,1)S(1)}, u32[]{:S(2)}, u32[]{:S(2)}) collective-permute-start(bf16[2,184,1024]{2,1,0:T(8,128)(2,1)} %get-tuple-element.128), channel_id=1, source_target_pairs={{0,6},{1,7},{2,4},{3,5},{4,2},{5,3},{6,0},{7,1},{8,14},{9,15},{10,... | collective-permute-start | bytes 2261000 | tf_op jit(solution)/shard_map/ppermute | solution.py:424
  121.3 34.4 %collective-permute-start.22 = (bf16[2,184,1024]{2,1,0:T(8,128)(2,1)}, bf16[2,184,1024]{2,1,0:T(8,128)(2,1)S(1)}, u32[]{:S(2)}, u32[]{:S(2)}) collective-permute-start(bf16[2,184,1024]{2,1,0:T(8,128)(2,1)} %get-tuple-element.124), channel_id=1, source_target_pairs={{0,2},{1,3},{2,0},{3,1},{4,6},{5,7},{6,4},{7,5},{8,10},{9,11},{10,... | collective-permute-start | bytes 2261000 | tf_op jit(solution)/shard_map/ppermute | solution.py:424
  123.2 33.3 %collective-permute-start.23 = (bf16[2,184,1024]{2,1,0:T(8,128)(2,1)S(1)}, bf16[2,184,1024]{2,1,0:T(8,128)(2,1)}, u32[]{:S(2)}, u32[]{:S(2)}) collective-permute-start(bf16[2,184,1024]{2,1,0:T(8,128)(2,1)S(1)} %copy-done.29), channel_id=1, source_target_pairs={{0,4},{1,5},{2,6},{3,7},{4,0},{5,1},{6,2},{7,3},{8,12},{9,13},{10,... | collective-permute-start | bytes 2261000 | tf_op jit(solution)/shard_map/ppermute | solution.py:424
  159.4 22.3 %collective-permute-start.27 = (bf16[4,184,1024]{2,1,0:T(8,128)(2,1)}, bf16[4,184,1024]{2,1,0:T(8,128)(2,1)S(1)}, u32[]{:S(2)}, u32[]{:S(2)}) collective-permute-start(bf16[4,184,1024]{2,1,0:T(8,128)(2,1)} %get-tuple-element.135), channel_id=1, source_target_pairs={{0,1},{1,0},{2,3},{3,2},{4,5},{5,4},{6,7},{7,6},{8,9},{9,8},{10,11... | collective-permute-start | bytes 4521992 | tf_op jit(solution)/shard_map/ppermute | solution.py:381
  161.0 33.6 %collective-permute-start.28 = (bf16[2,184,512]{2,1,0:T(8,128)(2,1)}, bf16[2,184,512]{2,1,0:T(8,128)(2,1)S(1)}, u32[]{:S(2)}, u32[]{:S(2)}) collective-permute-start(bf16[2,184,512]{2,1,0:T(8,128)(2,1)} %get-tuple-element.137), channel_id=1, source_target_pairs={{0,2},{1,3},{2,0},{3,1},{4,6},{5,7},{6,4},{7,5},{8,10},{9,11},{10,... | collective-permute-start | bytes 1130504 | tf_op jit(solution)/shard_map/ppermute | solution.py:424
  161.7 32.8 %collective-permute-start.29 = (bf16[2,184,512]{2,1,0:T(8,128)(2,1)}, bf16[2,184,512]{2,1,0:T(8,128)(2,1)S(1)}, u32[]{:S(2)}, u32[]{:S(2)}) collective-permute-start(bf16[2,184,512]{2,1,0:T(8,128)(2,1)} %get-tuple-element.139), channel_id=1, source_target_pairs={{0,4},{1,5},{2,6},{3,7},{4,0},{5,1},{6,2},{7,3},{8,12},{9,13},{10,... | collective-permute-start | bytes 1130504 | tf_op jit(solution)/shard_map/ppermute | solution.py:424
  165.3 29.3 %collective-permute-start.30 = (bf16[2,184,512]{2,1,0:T(8,128)(2,1)}, bf16[2,184,512]{2,1,0:T(8,128)(2,1)S(1)}, u32[]{:S(2)}, u32[]{:S(2)}) collective-permute-start(bf16[2,184,512]{2,1,0:T(8,128)(2,1)} %get-tuple-element.141), channel_id=1, source_target_pairs={{0,6},{1,7},{2,4},{3,5},{4,2},{5,3},{6,0},{7,1},{8,14},{9,15},{10,... | collective-permute-start | bytes 1130504 | tf_op jit(solution)/shard_map/ppermute | solution.py:424
  179.4 15.1 %collective-permute-start.21 = (bf16[180,320]{1,0:T(8,128)(2,1)}, bf16[180,320]{1,0:T(8,128)(2,1)S(1)}, u32[]{:S(2)}, u32[]{:S(2)}) collective-permute-start(bf16[180,320]{1,0:T(8,128)(2,1)} %get-tuple-element.122), channel_id=1, source_target_pairs={{8,0},{16,8},{24,16},{9,1},{17,9},{25,17},{10,2},{18,10},{26,18},{... | collective-permute-start | bytes 345608 | tf_op jit(solution)/shard_map/ppermute | solution.py:534
  (41 other events, 271.1 us)

commit v3 on v2

--- a/solution.py
+++ b/solution.py
@@ -207,7 +207,7 @@
     parts = refs[1:]
     block, tail, own_rows, field, result, block_sem, tail_sem, row_sem, out_sem = refs[-9:]
     me, polar = number(), in_polar_tile()
-    width = 15
+    width = 30
     groups = count // 2
     begin, end = span
     first, last = max(begin - 1, 0), min(end + 1, tiles)
@@ -486,9 +486,9 @@
         )
 
     up, mine = pack([helped, lone])
+    lifted = hop(*up, helpers)
     ys = select(apart(mine))
     got_lone = exchange(ys)
-    lifted = hop(*(tie(v, ys[0]) for v in up), helpers)
     own, mine = pack([shared, late])
     own, mine = apart(own), apart(mine)
     got = exchange(select(own, lifted, got_lone[1:]))

time: 218 us -> 216 us (level)
  waiting for transfers between devices: 76 us -> 73.1 us
    ppermute x2, waiting for transfers between devices: 13.1 us -> 7.5 us  [hop(): lax.ppermute(par, ('lat', 'lon'), crossed)]
    ppermute x18, waiting for transfers between devices: 38.9 us -> 44.4 us  [exchange(): lax.ppermute(value, 'lon', [(i, i ^ 2 * m) for i in range(count)])]
    ppermute x6, waiting for transfers between devices: 5.22 us -> 2.08 us  [swapped(): return lax.ppermute(value, 'lon', [(i, i ^ 1) for i in range(count)])]
    unnamed x67 -> x65, local copies, waits for them, and re-layouts: 10.1 us -> 10.4 us
  transfers between devices with their start and end apart: 32 -> 32, of which waited for: 17 -> 17; matrix products, arithmetic and copies ran while one was open for 2% -> 2% of each run, Pallas kernels for 25% -> 26%
where the time goes in v3:
time: 216 us; the launch traced here: 213 us
  Pallas kernels  80.8 us (37%)
  waiting for transfers between devices  73.1 us (34%)
  starting transfers between devices  43.7 us (20%)
  local copies, waits for them, and re-layouts  13.3 us (6%)
    pallas_call x13, Pallas kernels, call(): pl.pallas_call(kernel, in_specs=specs, out_specs=[ANY] * len(outs), out_s...  77.4 us
    ppermute x18, waiting for transfers between devices, exchange(): lax.ppermute(value, 'lon', [(i, i ^ 2 * m) for i in range(count)])  44.4 us
    ppermute x18, starting transfers between devices, exchange(): lax.ppermute(value, 'lon', [(i, i ^ 2 * m) for i in range(count)])  22.3 us
    ppermute x2, waiting for transfers between devices, hop(): lax.ppermute(own, 'lat', pairs)  15.1 us
    unnamed x65, local copies, waits for them, and re-layouts  10.4 us
    ppermute x2, waiting for transfers between devices, hop(): lax.ppermute(par, ('lat', 'lon'), crossed)  7.5 us
    ppermute x2, starting transfers between devices, hop(): lax.ppermute(par, ('lat', 'lon'), crossed)  5.92 us
    ppermute x1, starting transfers between devices, per_device(): lax.ppermute(last, 'lat', [(i, i + 1) for i in range(lats - 1)])  5.25 us
  transfers between devices with their start and end apart: 32, of which 17 were waited for; matrix products, arithmetic and copies ran while one was open for 2% of the time, Pallas kernels for 26%

profile of v3, /device:TPU:0, one launch (start us, length us, event | category | flops | bytes accessed | tf_op | source)
XLA Modules:
  0.0 213.3 jit_solution(10072755338965106647)
XLA Ops:
  0.0 5.6 %pack.2 = (bf16[4,184,512]{2,1,0:T(8,128)(2,1)}, bf16[4,184,512]{2,1,0:T(8,128)(2,1)}, bf16[4,184,1024]{2,1,0:T(8,128)(2,1)}, bf16[4,184,1024]{2,1,0:T(8,128)(2,1)}) custom-call(bf16[180,64,320]{2,1,0:T(8,128)(2,1)} %bitcast.5), custom_call_target="tpu_custom_call" | custom-call | flops 1 | bytes 1 | tf_op jit(solution)/shard_map/pack/pallas_call | solution.py:363
  6.1 4.6 %collective-permute-start.3 = (bf16[4,184,512]{2,1,0:T(8,128)(2,1)}, bf16[4,184,512]{2,1,0:T(8,128)(2,1)S(1)}, u32[]{:S(2)}, u32[]{:S(2)}) collective-permute-start(bf16[4,184,512]{2,1,0:T(8,128)(2,1)} %get-tuple-element.82), channel_id=1, source_target_pairs={{0,9},{1,8},{2,11},{3,10},{4,13},{5,12},{6,15},{7,14},{24,17},{25,... | collective-permute-start | bytes 2261000 | tf_op jit(solution)/shard_map/ppermute | solution.py:399
  11.9 2.9 %select.3 = (bf16[2,184,1024]{2,1,0:T(8,128)(2,1)}, bf16[2,184,1024]{2,1,0:T(8,128)(2,1)}, bf16[2,184,1024]{2,1,0:T(8,128)(2,1)}, bf16[2,184,1024]{2,1,0:T(8,128)(2,1)}) custom-call(bf16[4,184,1024]{2,1,0:T(8,128)(2,1)} %get-tuple-element.74.refs_0_, bf16[4,184,1024]{2,1,0:T(8,128)(2,1)} %copy-done.4), custom_call_target="tpu_custom_call" | custom-call | flops 1 | bytes 1 | tf_op jit(solution)/shard_map/select/pallas_call | solution.py:363
  16.4 3.4 %collective-permute-start.2 = (bf16[4,184,512]{2,1,0:T(8,128)(2,1)S(1)}, bf16[4,184,512]{2,1,0:T(8,128)(2,1)S(1)}, u32[]{:S(2)}, u32[]{:S(2)}) collective-permute-start(bf16[4,184,512]{2,1,0:T(8,128)(2,1)S(1)} %copy-done.30), channel_id=1, source_target_pairs={{0,8},{24,16},{1,9},{25,17},{2,10},{26,18},{3,11},{27,19},{4,12},{... | collective-permute-start | bytes 2261000 | tf_op jit(solution)/shard_map/ppermute | solution.py:399
  21.8 5.8 %pack.3 = (bf16[4,184,512]{2,1,0:T(8,128)(2,1)}, bf16[4,184,512]{2,1,0:T(8,128)(2,1)}, bf16[4,184,512]{2,1,0:T(8,128)(2,1)}, bf16[4,184,512]{2,1,0:T(8,128)(2,1)}) custom-call(bf16[180,64,320]{2,1,0:T(8,128)(2,1)} %bitcast.6), custom_call_target="tpu_custom_call" | custom-call | flops 1 | bytes 1 | tf_op jit(solution)/shard_map/pack/pallas_call | solution.py:363
  28.2 6.6 %collective-permute-done.4.refs_1_ = bf16[2,184,1024]{2,1,0:T(8,128)(2,1)S(1)} collective-permute-done((bf16[2,184,1024]{2,1,0:T(8,128)(2,1)}, bf16[2,184,1024]{2,1,0:T(8,128)(2,1)S(1)}, u32[]{:S(2)}, u32[]{:S(2)}) %collective-permute-start.4) | collective-permute-done | bytes 753696 | tf_op jit(solution)/shard_map/ppermute | solution.py:424
  35.7 18.9 %collective-permute-done.5.refs_2_ = bf16[2,184,1024]{2,1,0:T(8,128)(2,1)} collective-permute-done((bf16[2,184,1024]{2,1,0:T(8,128)(2,1)}, bf16[2,184,1024]{2,1,0:T(8,128)(2,1)}, u32[]{:S(2)}, u32[]{:S(2)}) %collective-permute-start.5) | collective-permute-done | bytes 753696 | tf_op jit(solution)/shard_map/ppermute | solution.py:424
  56.4 2.4 %select.4 = (bf16[2,184,512]{2,1,0:T(8,128)(2,1)}, bf16[2,184,512]{2,1,0:T(8,128)(2,1)}, bf16[2,184,512]{2,1,0:T(8,128)(2,1)}, bf16[2,184,512]{2,1,0:T(8,128)(2,1)}) custom-call(bf16[4,184,512]{2,1,0:T(8,128)(2,1)} %get-tuple-element.80.refs_0_, bf16[4,184,512]{2,1,0:T(8,128)(2,1)} %copy-done.11, bf16[4,184,512]{2,1,0:T(8,128)(2,1)} %copy-done.8, ...), custom_call_target="tpu_custom_call" | custom-call | flops 1 | bytes 1 | tf_op jit(solution)/shard_map/select/pallas_call | solution.py:363
  63.4 2.3 %select.5 = (bf16[2,184,512]{2,1,0:T(8,128)(2,1)}, bf16[2,184,512]{2,1,0:T(8,128)(2,1)}, bf16[2,184,512]{2,1,0:T(8,128)(2,1)}, bf16[2,184,512]{2,1,0:T(8,128)(2,1)}) custom-call(bf16[4,184,512]{2,1,0:T(8,128)(2,1)} %get-tuple-element.94.refs_0_, bf16[4,184,512]{2,1,0:T(8,128)(2,1)} %copy-done.6), custom_call_target="tpu_custom_call" | custom-call | flops 1 | bytes 1 | tf_op jit(solution)/shard_map/select/pallas_call | solution.py:363
  65.8 5.0 %collective-permute-done.7.refs_1_ = bf16[2,184,512]{2,1,0:T(8,128)(2,1)S(1)} collective-permute-done((bf16[2,184,512]{2,1,0:T(8,128)(2,1)}, bf16[2,184,512]{2,1,0:T(8,128)(2,1)S(1)}, u32[]{:S(2)}, u32[]{:S(2)}) %collective-permute-start.7) | collective-permute-done | bytes 376864 | tf_op jit(solution)/shard_map/ppermute | solution.py:424
  70.8 5.1 %collective-permute-done.8.refs_2_ = bf16[2,184,512]{2,1,0:T(8,128)(2,1)S(1)} collective-permute-done((bf16[2,184,512]{2,1,0:T(8,128)(2,1)}, bf16[2,184,512]{2,1,0:T(8,128)(2,1)S(1)}, u32[]{:S(2)}, u32[]{:S(2)}) %collective-permute-start.8) | collective-permute-done | bytes 376864 | tf_op jit(solution)/shard_map/ppermute | solution.py:424
  81.8 7.9 %filter.3 = (bf16[2,184,512]{2,1,0:T(8,128)(2,1)}, bf16[2,184,512]{2,1,0:T(8,128)(2,1)}, bf16[2,184,512]{2,1,0:T(8,128)(2,1)}, bf16[2,184,512]{2,1,0:T(8,128)(2,1)}) custom-call(s32[1,2048]{1,0:T(1,128)} %bitcast.14, bf16[2,184,512]{2,1,0:T(8,128)(2,1)} %get-tuple-element.87.refs_0_, bf16[2,184,512]{2,1,0:T(8,128)(2,1)} %copy-done.14, ...), custom_call_target="tpu_custom_call" | custom-call | flops 1 | bytes 1 | tf_op jit(solution)/shard_map/filter/pallas_call | solution.py:363
  92.2 4.8 %collective-permute-done.13.refs_2_ = bf16[2,184,512]{2,1,0:T(8,128)(2,1)S(1)} collective-permute-done((bf16[2,184,512]{2,1,0:T(8,128)(2,1)}, bf16[2,184,512]{2,1,0:T(8,128)(2,1)S(1)}, u32[]{:S(2)}, u32[]{:S(2)}) %collective-permute-start.13) | collective-permute-done | bytes 376864 | tf_op jit(solution)/shard_map/ppermute | solution.py:424
  100.2 11.7 %filter.4 = (bf16[2,184,1024]{2,1,0:T(8,128)(2,1)}, bf16[2,184,1024]{2,1,0:T(8,128)(2,1)}, bf16[2,184,1024]{2,1,0:T(8,128)(2,1)}, bf16[2,184,1024]{2,1,0:T(8,128)(2,1)}) custom-call(s32[1,2048]{1,0:T(1,128)} %bitcast.15, bf16[2,184,1024]{2,1,0:T(8,128)(2,1)} %get-tuple-element.78.refs_0_, bf16[2,184,1024]{2,1,0:T(8,128)(2,1)} %copy-done.12, ...), custom_call_target="tpu_custom_call" | custom-call | flops 1 | bytes 1 | tf_op jit(solution)/shard_map/filter/pallas_call | solution.py:363
  113.6 2.3 %gather.3 = (bf16[4,184,512]{2,1,0:T(8,128)(2,1)}, bf16[4,184,512]{2,1,0:T(8,128)(2,1)}) custom-call(bf16[2,184,512]{2,1,0:T(8,128)(2,1)} %get-tuple-element.99.refs_0_, bf16[2,184,512]{2,1,0:T(8,128)(2,1)} %copy-done.25, bf16[2,184,512]{2,1,0:T(8,128)(2,1)} %copy-done.24, bf16[2,184,512]{2,1,0:T(8,128)(2,1)} %copy-done.23), custom_call_target="tpu_custom_call" | custom-call | flops 1 | bytes 1 | tf_op jit(solution)/shard_map/gather/pallas_call | solution.py:363
  122.2 7.9 %filter.5 = (bf16[2,184,512]{2,1,0:T(8,128)(2,1)}, bf16[2,184,512]{2,1,0:T(8,128)(2,1)}, bf16[2,184,512]{2,1,0:T(8,128)(2,1)}, bf16[2,184,512]{2,1,0:T(8,128)(2,1)}) custom-call(s32[1,2048]{1,0:T(1,128)} %bitcast.16, bf16[2,184,512]{2,1,0:T(8,128)(2,1)} %get-tuple-element.97.refs_0_, bf16[2,184,512]{2,1,0:T(8,128)(2,1)} %copy-done.19, ...), custom_call_target="tpu_custom_call" | custom-call | flops 1 | bytes 1 | tf_op jit(solution)/shard_map/filter/pallas_call | solution.py:363
  130.1 7.0 %collective-permute-done.18.fp.lp.refs_4_ = bf16[4,184,512]{2,1,0:T(8,128)(2,1)S(1)} collective-permute-done((bf16[4,184,512]{2,1,0:T(8,128)(2,1)}, bf16[4,184,512]{2,1,0:T(8,128)(2,1)S(1)}, u32[]{:S(2)}, u32[]{:S(2)}) %collective-permute-start.18) | collective-permute-done | bytes 753696 | tf_op jit(solution)/shard_map/ppermute | solution.py:399
  137.0 15.1 %collective-permute-done.17.fo.lo.refs_3_ = bf16[4,184,512]{2,1,0:T(8,128)(2,1)S(1)} collective-permute-done((bf16[4,184,512]{2,1,0:T(8,128)(2,1)}, bf16[4,184,512]{2,1,0:T(8,128)(2,1)S(1)}, u32[]{:S(2)}, u32[]{:S(2)}) %collective-permute-start.17) | collective-permute-done | bytes 753696 | tf_op jit(solution)/shard_map/ppermute | solution.py:399
  154.5 2.8 %gather.4 = (bf16[4,184,1024]{2,1,0:T(8,128)(2,1)}, bf16[4,184,1024]{2,1,0:T(8,128)(2,1)}) custom-call(bf16[2,184,1024]{2,1,0:T(8,128)(2,1)} %get-tuple-element.113.refs_0_, bf16[2,184,1024]{2,1,0:T(8,128)(2,1)} %copy-done.10, bf16[2,184,1024]{2,1,0:T(8,128)(2,1)} %collective-permute-done.23.refs_2_, bf16[2,184,1024]{2,1,0:T(8,128)(2,1)} %copy-done.9), custom_call_target="tpu_custom_call" | custom-call | flops 1 | bytes 1 | tf_op jit(solution)/shard_map/gather/pallas_call | solution.py:363
  164.2 3.4 %edges.1 = (bf16[180,320]{1,0:T(8,128)(2,1)}, bf16[180,320]{1,0:T(8,128)(2,1)}) custom-call(bf16[4,184,512]{2,1,0:T(8,128)(2,1)} %copy-done.1, bf16[4,184,512]{2,1,0:T(8,128)(2,1)} %copy-done, bf16[4,184,512]{2,1,0:T(8,128)(2,1)} %copy-done.1, bf16[4,184,512]{2,1,0:T(8,128)(2,1)} %copy-done, bf16[4,184,512]{2,1,0:T(8,128)(2,1)} %get-tuple-element.115.fto.lto.refs_1_, ...), custom_call_target="tpu_custom_call" | custom-call | flops 1 | bytes 1 | tf_op jit(solution)/shard_map/edges/pallas_call | solution.py:523
  169.4 5.2 %collective-permute-start.20 = (bf16[180,320]{1,0:T(8,128)(2,1)}, bf16[180,320]{1,0:T(8,128)(2,1)S(1)}, u32[]{:S(2)}, u32[]{:S(2)}) collective-permute-start(bf16[180,320]{1,0:T(8,128)(2,1)} %get-tuple-element.117), channel_id=1, source_target_pairs={{0,8},{8,16},{16,24},{1,9},{9,17},{17,25},{2,10},{10,18},{18,26},{... | collective-permute-start | bytes 345608 | tf_op jit(solution)/shard_map/ppermute | solution.py:533
  180.9 11.5 %flux_step.2.refs_9_ = f32[180,64,320]{2,1,0:T(8,128)} custom-call(bf16[180,1,320]{2,1,0:T(2,128)(2,1)} %copy.17.north.south, bf16[180,1,320]{2,1,0:T(2,128)(2,1)} %copy.17.north.south, bf16[2,64,320]{2,1,0:T(8,128)(2,1)} %copy-done.13, f32[4,64,320]{2,1,0:T(8,128)} %pad_maximum_fusion.coef, bf16[180,64,320]{2,1,0:T(8,128)(2,1)} %bitcast.10, ...), custom_call_target="tpu_custom_call" | custom-call | flops 1 | bytes 1 | tf_op jit(solution)/shard_map/flux_step/pallas_call | solution.py:363
  194.1 2.3 %gather.5 = (bf16[4,184,512]{2,1,0:T(8,128)(2,1)}, bf16[4,184,512]{2,1,0:T(8,128)(2,1)}) custom-call(bf16[2,184,512]{2,1,0:T(8,128)(2,1)} %get-tuple-element.126.refs_0_, bf16[2,184,512]{2,1,0:T(8,128)(2,1)} %copy-done.20, bf16[2,184,512]{2,1,0:T(8,128)(2,1)} %copy-done.21, bf16[2,184,512]{2,1,0:T(8,128)(2,1)} %copy-done.22), custom_call_target="tpu_custom_call" | custom-call | flops 1 | bytes 1 | tf_op jit(solution)/shard_map/gather/pallas_call | solution.py:363
  201.1 12.1 %flux_step.3 = f32[180,64,320]{2,1,0:T(8,128)} custom-call(bf16[180,1,320]{2,1,0:T(2,128)(2,1)} %copy.17.north.south, bf16[180,1,320]{2,1,0:T(2,128)(2,1)} %copy.18.south, bf16[2,64,320]{2,1,0:T(8,128)(2,1)} %copy-done.13, f32[4,64,320]{2,1,0:T(8,128)} %pad_maximum_fusion.coef, bf16[180,64,320]{2,1,0:T(8,128)(2,1)} %bitcast.11, ...), custom_call_target="tpu_custom_call", output_to_operand_aliasing={{}: (13, {})} | custom-call | flops 1 | bytes 1 | tf_op jit(solution)/shard_map/flux_step/pallas_call | solution.py:363
  (134 shorter events, 56.1 us)
Async XLA Ops:
  6.1 22.1 %collective-permute-start.3 = (bf16[4,184,512]{2,1,0:T(8,128)(2,1)}, bf16[4,184,512]{2,1,0:T(8,128)(2,1)S(1)}, u32[]{:S(2)}, u32[]{:S(2)}) collective-permute-start(bf16[4,184,512]{2,1,0:T(8,128)(2,1)} %get-tuple-element.82), channel_id=1, source_target_pairs={{0,9},{1,8},{2,11},{3,10},{4,13},{5,12},{6,15},{7,14},{24,17},{25,... | collective-permute-start | bytes 2261000 | tf_op jit(solution)/shard_map/ppermute | solution.py:399
  14.8 20.0 %collective-permute-start.4 = (bf16[2,184,1024]{2,1,0:T(8,128)(2,1)}, bf16[2,184,1024]{2,1,0:T(8,128)(2,1)S(1)}, u32[]{:S(2)}, u32[]{:S(2)}) collective-permute-start(bf16[2,184,1024]{2,1,0:T(8,128)(2,1)} %get-tuple-element.83), channel_id=1, source_target_pairs={{0,2},{1,3},{2,0},{3,1},{4,6},{5,7},{6,4},{7,5},{8,10},{9,11},{10,... | collective-permute-start | bytes 2261000 | tf_op jit(solution)/shard_map/ppermute | solution.py:424
  16.4 38.3 %collective-permute-start.2 = (bf16[4,184,512]{2,1,0:T(8,128)(2,1)S(1)}, bf16[4,184,512]{2,1,0:T(8,128)(2,1)S(1)}, u32[]{:S(2)}, u32[]{:S(2)}) collective-permute-start(bf16[4,184,512]{2,1,0:T(8,128)(2,1)S(1)} %copy-done.30), channel_id=1, source_target_pairs={{0,8},{24,16},{1,9},{25,17},{2,10},{26,18},{3,11},{27,19},{4,12},{... | collective-permute-start | bytes 2261000 | tf_op jit(solution)/shard_map/ppermute | solution.py:399
  19.8 34.9 %collective-permute-start.5 = (bf16[2,184,1024]{2,1,0:T(8,128)(2,1)}, bf16[2,184,1024]{2,1,0:T(8,128)(2,1)}, u32[]{:S(2)}, u32[]{:S(2)}) collective-permute-start(bf16[2,184,1024]{2,1,0:T(8,128)(2,1)} %get-tuple-element.84), channel_id=1, source_target_pairs={{0,4},{1,5},{2,6},{3,7},{4,0},{5,1},{6,2},{7,3},{8,12},{9,13},{10,... | collective-permute-start | bytes 2261000 | tf_op jit(solution)/shard_map/ppermute | solution.py:424
  21.3 33.3 %collective-permute-start.6 = (bf16[2,184,1024]{2,1,0:T(8,128)(2,1)}, bf16[2,184,1024]{2,1,0:T(8,128)(2,1)}, u32[]{:S(2)}, u32[]{:S(2)}) collective-permute-start(bf16[2,184,1024]{2,1,0:T(8,128)(2,1)} %get-tuple-element.85), channel_id=1, source_target_pairs={{0,6},{1,7},{2,4},{3,5},{4,2},{5,3},{6,0},{7,1},{8,14},{9,15},{10,... | collective-permute-start | bytes 2261000 | tf_op jit(solution)/shard_map/ppermute | solution.py:424
  28.2 26.5 %collective-permute-start.1 = (bf16[4,184,512]{2,1,0:T(8,128)(2,1)}, bf16[4,184,512]{2,1,0:T(8,128)(2,1)S(1)}, u32[]{:S(2)}, u32[]{:S(2)}) collective-permute-start(bf16[4,184,512]{2,1,0:T(8,128)(2,1)} %get-tuple-element.81), channel_id=1, source_target_pairs={{0,1},{1,0},{2,3},{3,2},{4,5},{5,4},{6,7},{7,6},{8,9},{9,8},{10,11... | collective-permute-start | bytes 2261000 | tf_op jit(solution)/shard_map/ppermute | solution.py:381
  35.7 26.9 %collective-permute-start.10 = (bf16[4,184,512]{2,1,0:T(8,128)(2,1)}, bf16[4,184,512]{2,1,0:T(8,128)(2,1)S(1)}, u32[]{:S(2)}, u32[]{:S(2)}) collective-permute-start(bf16[4,184,512]{2,1,0:T(8,128)(2,1)} %get-tuple-element.95), channel_id=1, source_target_pairs={{0,1},{1,0},{2,3},{3,2},{4,5},{5,4},{6,7},{7,6},{8,9},{9,8},{10,11... | collective-permute-start | bytes 2261000 | tf_op jit(solution)/shard_map/ppermute | solution.py:381
  59.4 16.5 %collective-permute-start.8 = (bf16[2,184,512]{2,1,0:T(8,128)(2,1)}, bf16[2,184,512]{2,1,0:T(8,128)(2,1)S(1)}, u32[]{:S(2)}, u32[]{:S(2)}) collective-permute-start(bf16[2,184,512]{2,1,0:T(8,128)(2,1)} %get-tuple-element.91), channel_id=1, source_target_pairs={{0,4},{1,5},{2,6},{3,7},{4,0},{5,1},{6,2},{7,3},{8,12},{9,13},{10,... | collective-permute-start | bytes 1130504 | tf_op jit(solution)/shard_map/ppermute | solution.py:424
  61.0 16.5 %collective-permute-start.9 = (bf16[2,184,512]{2,1,0:T(8,128)(2,1)}, bf16[2,184,512]{2,1,0:T(8,128)(2,1)S(1)}, u32[]{:S(2)}, u32[]{:S(2)}) collective-permute-start(bf16[2,184,512]{2,1,0:T(8,128)(2,1)} %get-tuple-element.93), channel_id=1, source_target_pairs={{0,6},{1,7},{2,4},{3,5},{4,2},{5,3},{6,0},{7,1},{8,14},{9,15},{10,... | collective-permute-start | bytes 1130504 | tf_op jit(solution)/shard_map/ppermute | solution.py:424
  77.5 12.8 %collective-permute-start.15 = (bf16[2,184,512]{2,1,0:T(8,128)(2,1)}, bf16[2,184,512]{2,1,0:T(8,128)(2,1)S(1)}, u32[]{:S(2)}, u32[]{:S(2)}) collective-permute-start(bf16[2,184,512]{2,1,0:T(8,128)(2,1)} %get-tuple-element.110), channel_id=1, source_target_pairs={{0,6},{1,7},{2,4},{3,5},{4,2},{5,3},{6,0},{7,1},{8,14},{9,15},{10,... | collective-permute-start | bytes 1130504 | tf_op jit(solution)/shard_map/ppermute | solution.py:424
  79.3 17.7 %collective-permute-start.13 = (bf16[2,184,512]{2,1,0:T(8,128)(2,1)}, bf16[2,184,512]{2,1,0:T(8,128)(2,1)S(1)}, u32[]{:S(2)}, u32[]{:S(2)}) collective-permute-start(bf16[2,184,512]{2,1,0:T(8,128)(2,1)} %get-tuple-element.106), channel_id=1, source_target_pairs={{0,4},{1,5},{2,6},{3,7},{4,0},{5,1},{6,2},{7,3},{8,12},{9,13},{10,... | collective-permute-start | bytes 1130504 | tf_op jit(solution)/shard_map/ppermute | solution.py:424
  79.8 19.4 %collective-permute-start.11 = (bf16[2,184,512]{2,1,0:T(8,128)(2,1)}, bf16[2,184,512]{2,1,0:T(8,128)(2,1)S(1)}, u32[]{:S(2)}, u32[]{:S(2)}) collective-permute-start(bf16[2,184,512]{2,1,0:T(8,128)(2,1)} %get-tuple-element.102), channel_id=1, source_target_pairs={{0,2},{1,3},{2,0},{3,1},{4,6},{5,7},{6,4},{7,5},{8,10},{9,11},{10,... | collective-permute-start | bytes 1130504 | tf_op jit(solution)/shard_map/ppermute | solution.py:424
  90.3 21.6 %collective-permute-start.16 = (bf16[2,184,512]{2,1,0:T(8,128)(2,1)}, bf16[2,184,512]{2,1,0:T(8,128)(2,1)S(1)}, u32[]{:S(2)}, u32[]{:S(2)}) collective-permute-start(bf16[2,184,512]{2,1,0:T(8,128)(2,1)} %get-tuple-element.111), channel_id=1, source_target_pairs={{0,6},{1,7},{2,4},{3,5},{4,2},{5,3},{6,0},{7,1},{8,14},{9,15},{10,... | collective-permute-start | bytes 1130504 | tf_op jit(solution)/shard_map/ppermute | solution.py:424
  97.0 15.0 %collective-permute-start.14 = (bf16[2,184,512]{2,1,0:T(8,128)(2,1)}, bf16[2,184,512]{2,1,0:T(8,128)(2,1)S(1)}, u32[]{:S(2)}, u32[]{:S(2)}) collective-permute-start(bf16[2,184,512]{2,1,0:T(8,128)(2,1)} %get-tuple-element.107), channel_id=1, source_target_pairs={{0,4},{1,5},{2,6},{3,7},{4,0},{5,1},{6,2},{7,3},{8,12},{9,13},{10,... | collective-permute-start | bytes 1130504 | tf_op jit(solution)/shard_map/ppermute | solution.py:424
  115.8 21.2 %collective-permute-start.18 = (bf16[4,184,512]{2,1,0:T(8,128)(2,1)}, bf16[4,184,512]{2,1,0:T(8,128)(2,1)S(1)}, u32[]{:S(2)}, u32[]{:S(2)}) collective-permute-start(bf16[4,184,512]{2,1,0:T(8,128)(2,1)} %get-tuple-element.116), channel_id=1, source_target_pairs={{8,1},{9,0},{10,3},{11,2},{12,5},{13,4},{14,7},{15,6},{16,25},{17,... | collective-permute-start | bytes 2261000 | tf_op jit(solution)/shard_map/ppermute | solution.py:399
  117.1 35.0 %collective-permute-start.17 = (bf16[4,184,512]{2,1,0:T(8,128)(2,1)}, bf16[4,184,512]{2,1,0:T(8,128)(2,1)S(1)}, u32[]{:S(2)}, u32[]{:S(2)}) collective-permute-start(bf16[4,184,512]{2,1,0:T(8,128)(2,1)} %get-tuple-element.115.fto.lto.refs_1_), channel_id=1, source_target_pairs={{8,0},{16,24},{9,1},{17,25},{10,2},{18,26},{11,3},{19,27},{12,4},{... | collective-permute-start | bytes 2261000 | tf_op jit(solution)/shard_map/ppermute | solution.py:399
  118.6 33.5 %collective-permute-start.24 = (bf16[2,184,1024]{2,1,0:T(8,128)(2,1)}, bf16[2,184,1024]{2,1,0:T(8,128)(2,1)S(1)}, u32[]{:S(2)}, u32[]{:S(2)}) collective-permute-start(bf16[2,184,1024]{2,1,0:T(8,128)(2,1)} %get-tuple-element.124), channel_id=1, source_target_pairs={{0,6},{1,7},{2,4},{3,5},{4,2},{5,3},{6,0},{7,1},{8,14},{9,15},{10,... | collective-permute-start | bytes 2261000 | tf_op jit(solution)/shard_map/ppermute | solution.py:424
  119.2 34.4 %collective-permute-start.22 = (bf16[2,184,1024]{2,1,0:T(8,128)(2,1)}, bf16[2,184,1024]{2,1,0:T(8,128)(2,1)S(1)}, u32[]{:S(2)}, u32[]{:S(2)}) collective-permute-start(bf16[2,184,1024]{2,1,0:T(8,128)(2,1)} %get-tuple-element.120), channel_id=1, source_target_pairs={{0,2},{1,3},{2,0},{3,1},{4,6},{5,7},{6,4},{7,5},{8,10},{9,11},{10,... | collective-permute-start | bytes 2261000 | tf_op jit(solution)/shard_map/ppermute | solution.py:424
  121.1 32.9 %collective-permute-start.23 = (bf16[2,184,1024]{2,1,0:T(8,128)(2,1)S(1)}, bf16[2,184,1024]{2,1,0:T(8,128)(2,1)}, u32[]{:S(2)}, u32[]{:S(2)}) collective-permute-start(bf16[2,184,1024]{2,1,0:T(8,128)(2,1)S(1)} %copy-done.29), channel_id=1, source_target_pairs={{0,4},{1,5},{2,6},{3,7},{4,0},{5,1},{6,2},{7,3},{8,12},{9,13},{10,... | collective-permute-start | bytes 2261000 | tf_op jit(solution)/shard_map/ppermute | solution.py:424
  157.3 22.5 %collective-permute-start.27 = (bf16[4,184,1024]{2,1,0:T(8,128)(2,1)}, bf16[4,184,1024]{2,1,0:T(8,128)(2,1)S(1)}, u32[]{:S(2)}, u32[]{:S(2)}) collective-permute-start(bf16[4,184,1024]{2,1,0:T(8,128)(2,1)} %get-tuple-element.131), channel_id=1, source_target_pairs={{0,1},{1,0},{2,3},{3,2},{4,5},{5,4},{6,7},{7,6},{8,9},{9,8},{10,11... | collective-permute-start | bytes 4521992 | tf_op jit(solution)/shard_map/ppermute | solution.py:381
  158.9 33.6 %collective-permute-start.28 = (bf16[2,184,512]{2,1,0:T(8,128)(2,1)}, bf16[2,184,512]{2,1,0:T(8,128)(2,1)S(1)}, u32[]{:S(2)}, u32[]{:S(2)}) collective-permute-start(bf16[2,184,512]{2,1,0:T(8,128)(2,1)} %get-tuple-element.133), channel_id=1, source_target_pairs={{0,2},{1,3},{2,0},{3,1},{4,6},{5,7},{6,4},{7,5},{8,10},{9,11},{10,... | collective-permute-start | bytes 1130504 | tf_op jit(solution)/shard_map/ppermute | solution.py:424
  159.7 32.8 %collective-permute-start.29 = (bf16[2,184,512]{2,1,0:T(8,128)(2,1)}, bf16[2,184,512]{2,1,0:T(8,128)(2,1)S(1)}, u32[]{:S(2)}, u32[]{:S(2)}) collective-permute-start(bf16[2,184,512]{2,1,0:T(8,128)(2,1)} %get-tuple-element.135), channel_id=1, source_target_pairs={{0,4},{1,5},{2,6},{3,7},{4,0},{5,1},{6,2},{7,3},{8,12},{9,13},{10,... | collective-permute-start | bytes 1130504 | tf_op jit(solution)/shard_map/ppermute | solution.py:424
  163.4 29.1 %collective-permute-start.30 = (bf16[2,184,512]{2,1,0:T(8,128)(2,1)}, bf16[2,184,512]{2,1,0:T(8,128)(2,1)S(1)}, u32[]{:S(2)}, u32[]{:S(2)}) collective-permute-start(bf16[2,184,512]{2,1,0:T(8,128)(2,1)} %get-tuple-element.137), channel_id=1, source_target_pairs={{0,6},{1,7},{2,4},{3,5},{4,2},{5,3},{6,0},{7,1},{8,14},{9,15},{10,... | collective-permute-start | bytes 1130504 | tf_op jit(solution)/shard_map/ppermute | solution.py:424
  177.5 14.9 %collective-permute-start.21 = (bf16[180,320]{1,0:T(8,128)(2,1)}, bf16[180,320]{1,0:T(8,128)(2,1)S(1)}, u32[]{:S(2)}, u32[]{:S(2)}) collective-permute-start(bf16[180,320]{1,0:T(8,128)(2,1)} %get-tuple-element.118), channel_id=1, source_target_pairs={{8,0},{16,8},{24,16},{9,1},{17,9},{25,17},{10,2},{18,10},{26,18},{... | collective-permute-start | bytes 345608 | tf_op jit(solution)/shard_map/ppermute | solution.py:534
  (40 other events, 270.0 us)
